TPU v7x, 512 devices: a whole 4x4x16 slice. The times are simulated.
512 devices in a mesh: dp: 8 (over z_lo, core), context: 64 (over y, x, z_hi).
Axes of the slice: x: 4, y: 4, z: 16 (z_hi: 4, z_lo: 4; z = z_hi * 4 + z_lo), core: 2. Of those that a mesh axis runs over, the one named last changes fastest.
Arguments:
- value: bfloat16 [1, 4096, 8192], P(None, 'dp', 'context'), may hold values from -6 to 6
- key_one: bfloat16 [1, 4096, 8192], P(None, 'dp', 'context'), may hold values from -6 to 6
- gate_one: bfloat16 [1, 4096, 8192], P(None, 'dp', 'context'), may hold values from -6 to 6
- conv_one: bfloat16 [1, 4096, 8192], P(None, 'dp', 'context'), may hold values from -6 to 6
- key_two: bfloat16 [1, 4096, 8192], P(None, 'dp', 'context'), may hold values from -6 to 6
- gate_two: bfloat16 [1, 4096, 8192], P(None, 'dp', 'context'), may hold values from -6 to 6
- conv_two: bfloat16 [1, 4096, 8192], P(None, 'dp', 'context'), may hold values from -6 to 6
- grad_out: bfloat16 [1, 4096, 8192], P(None, 'dp', 'context'), may hold values from -16 to 16
- residues_one: float32 [4096, 16], P('dp'), may hold values from -3 to 3
- log_rate_one: float32 [4096, 16], P('dp'), may hold values from -16 to -3
- residues_two: float32 [4096, 16], P('dp'), may hold values from -3 to 3
- log_rate_two: float32 [4096, 16], P('dp'), may hold values from -16 to -3
Outputs:
- grad_value: bfloat16 [1, 4096, 8192], P(None, 'dp', 'context')
- grad_key_one: bfloat16 [1, 4096, 8192], P(None, 'dp', 'context')
- grad_gate_one: bfloat16 [1, 4096, 8192], P(None, 'dp', 'context')
- grad_key_two: bfloat16 [1, 4096, 8192], P(None, 'dp', 'context')
- grad_gate_two: bfloat16 [1, 4096, 8192], P(None, 'dp', 'context')
- grad_residues_one: float32 [4096, 16], P('dp')
- grad_log_rate_one: float32 [4096, 16], P('dp')
- grad_residues_two: float32 [4096, 16], P('dp')
- grad_log_rate_two: float32 [4096, 16], P('dp')
All inputs are finite; a program needn't handle non-finite values.
Results may differ from a plain program's by a relative error of at most 0.0022.
Values sent between devices are 32-bit elements; how exact they have to be, the bound alone decides.
A program may use at most 128 MiB of HBM per device.

v0:
```python
from functools import partial
import math

import jax
import jax.numpy as jnp
from jax import lax
from jax.sharding import PartitionSpec as P

ROW = 128


def local_filter(residues, log_rate, positions):
    rate = jnp.exp(log_rate)
    amplitude = residues * jnp.sqrt(2.0 * rate)
    decay = jnp.exp(-rate[:, :, None] * positions[None, None, :])
    return jnp.sum(amplitude[:, :, None] * decay, axis=1)


def angles(left, right, length):
    product = left[:, None] * right[None, :] % length
    return product.astype(jnp.float32) * (2.0 * math.pi / length)


def matmul(form, left, right):
    return jnp.einsum(
        form, left, right, precision=lax.Precision.HIGHEST, preferred_element_type=jnp.float32
    )


def widen(array):
    return array.astype(jnp.float32)


def take(pair, start, count):
    return (pair[0][start : start + count], pair[1][start : start + count])


def per_device(
    value,
    key_one,
    gate_one,
    conv_one,
    key_two,
    gate_two,
    conv_two,
    grad_out,
    residues_one,
    log_rate_one,
    residues_two,
    log_rate_two,
):
    parts = lax.axis_size("context")
    place = lax.axis_index("context")
    batch_here, channels, local = value.shape
    flat = batch_here * channels
    through = widen(gate_one) * widen(conv_one)
    signal_two = widen(key_two) * through
    signal_one = widen(key_one) * widen(value)
    grad_gate_two = (widen(grad_out) * widen(conv_two)).astype(jnp.bfloat16)
    source_two = widen(grad_out) * widen(gate_two)
    width = ROW
    total = 2 * local * parts
    tall = total // width
    half = tall // 2
    own_rows = local // width
    own_cols = width // parts
    own_freq = tall // parts
    positions = (place * local + jnp.arange(local, dtype=jnp.int32)).astype(jnp.float32)
    ramp_tall = jnp.arange(tall, dtype=jnp.int32)
    ramp_wide = jnp.arange(width, dtype=jnp.int32)
    first_angle = angles(jnp.arange(half, dtype=jnp.int32), ramp_tall, tall)
    first_cos = jnp.cos(first_angle)
    first_sin = jnp.sin(first_angle)
    wide_angle = angles(ramp_wide, ramp_wide, width)
    wide_cos = jnp.cos(wide_angle)
    wide_sin = jnp.sin(wide_angle)
    fwd_angle = angles(place * own_cols + jnp.arange(own_cols, dtype=jnp.int32), ramp_tall, total)
    fwd_cos = jnp.cos(fwd_angle)
    fwd_sin = jnp.sin(fwd_angle)
    inv_angle = angles(place * own_freq + jnp.arange(own_freq, dtype=jnp.int32), ramp_wide, total)
    inv_cos = jnp.cos(inv_angle)
    inv_sin = jnp.sin(inv_angle)

    def first_section(gathered):
        real = matmul("rmj,mk->rjk", gathered, first_cos)
        imag = -matmul("rmj,mk->rjk", gathered, first_sin)
        return (real * fwd_cos + imag * fwd_sin, imag * fwd_cos - real * fwd_sin)

    def second_section(pieces):
        real, imag = pieces
        real_cos = matmul("rnk,nq->rkq", real, wide_cos)
        real_sin = matmul("rnk,nq->rkq", real, wide_sin)
        imag_cos = matmul("rnk,nq->rkq", imag, wide_cos)
        imag_sin = matmul("rnk,nq->rkq", imag, wide_sin)
        return (real_cos + imag_sin, imag_cos - real_sin)

    def forward(signal):
        block = signal.reshape(signal.shape[0], own_rows, width)
        spread = first_section(
            lax.all_to_all(block, "context", split_axis=2, concat_axis=1, tiled=True)
        )
        return second_section(
            (
                lax.all_to_all(spread[0], "context", split_axis=2, concat_axis=1, tiled=True),
                lax.all_to_all(spread[1], "context", split_axis=2, concat_axis=1, tiled=True),
            )
        )

    def final_section(pieces):
        real, imag = pieces
        summed = matmul("rkj,nk->rnj", real, first_cos) - matmul("rkj,nk->rnj", imag, first_sin)
        return summed / total

    def inverse(real, imag):
        real_cos = matmul("rkq,qn->rkn", real, wide_cos)
        real_sin = matmul("rkq,qn->rkn", real, wide_sin)
        imag_cos = matmul("rkq,qn->rkn", imag, wide_cos)
        imag_sin = matmul("rkq,qn->rkn", imag, wide_sin)
        part_real = real_cos - imag_sin
        part_imag = imag_cos + real_sin
        twisted_real = part_real * inv_cos - part_imag * inv_sin
        twisted_imag = part_imag * inv_cos + part_real * inv_sin
        mixed = final_section(
            (
                lax.all_to_all(twisted_real, "context", split_axis=2, concat_axis=1, tiled=True),
                lax.all_to_all(twisted_imag, "context", split_axis=2, concat_axis=1, tiled=True),
            )
        )
        placed = lax.all_to_all(mixed, "context", split_axis=1, concat_axis=2, tiled=True)
        return placed.reshape(placed.shape[0], local)

    def backward(source_spec, signal_spec, filter_spec):
        shape = (batch_here, channels, own_freq, width)
        src_real = source_spec[0].reshape(shape)
        src_imag = source_spec[1].reshape(shape)
        sig_real = signal_spec[0].reshape(shape)
        sig_imag = signal_spec[1].reshape(shape)
        filt_real = filter_spec[0][None]
        filt_imag = filter_spec[1][None]
        back_real = filt_real * src_real + filt_imag * src_imag
        back_imag = filt_real * src_imag - filt_imag * src_real
        fgrad_real = jnp.sum(src_real * sig_real + src_imag * sig_imag, axis=0)
        fgrad_imag = jnp.sum(src_imag * sig_real - src_real * sig_imag, axis=0)
        stacked_real = jnp.concatenate(
            [back_real.reshape(flat, own_freq, width), fgrad_real], axis=0
        )
        stacked_imag = jnp.concatenate(
            [back_imag.reshape(flat, own_freq, width), fgrad_imag], axis=0
        )
        result = inverse(stacked_real, stacked_imag)
        return (result[:flat].reshape(batch_here, channels, local), result[flat:])

    filter_one, pull_one = jax.vjp(
        partial(local_filter, positions=positions), residues_one, log_rate_one
    )
    filter_two, pull_two = jax.vjp(
        partial(local_filter, positions=positions), residues_two, log_rate_two
    )
    spectra = forward(
        jnp.concatenate(
            [source_two.reshape(flat, local), signal_two.reshape(flat, local), filter_two], axis=0
        )
    )
    back_two, fgrad_two = backward(
        take(spectra, 0, flat), take(spectra, flat, flat), take(spectra, 2 * flat, channels)
    )
    grad_key_two = (back_two * through).astype(jnp.bfloat16)
    grad_through = back_two * widen(key_two)
    grad_gate_one = (grad_through * widen(conv_one)).astype(jnp.bfloat16)
    source_one = grad_through * widen(gate_one)
    later = forward(
        jnp.concatenate(
            [source_one.reshape(flat, local), signal_one.reshape(flat, local), filter_one], axis=0
        )
    )
    back_one, fgrad_one = backward(
        take(later, 0, flat), take(later, flat, flat), take(later, 2 * flat, channels)
    )
    res_one, log_one = pull_one(fgrad_one)
    res_two, log_two = pull_two(fgrad_two)
    grad_key_one = (back_one * widen(value)).astype(jnp.bfloat16)
    grad_value = (back_one * widen(key_one)).astype(jnp.bfloat16)
    summed = lax.psum((res_one, log_one, res_two, log_two), "context")
    scale = 1.0 / math.sqrt(batch_here * local * parts)
    return (
        grad_value,
        grad_key_one,
        grad_gate_one,
        grad_key_two,
        grad_gate_two,
        summed[0] * scale,
        summed[1] * scale,
        summed[2] * scale,
        summed[3] * scale,
    )


def solution(mesh):
    in_specs = (
        P(None, "dp", "context"),
        P(None, "dp", "context"),
        P(None, "dp", "context"),
        P(None, "dp", "context"),
        P(None, "dp", "context"),
        P(None, "dp", "context"),
        P(None, "dp", "context"),
        P(None, "dp", "context"),
        P("dp", None),
        P("dp", None),
        P("dp", None),
        P("dp", None),
    )
    out_specs = (
        P(None, "dp", "context"),
        P(None, "dp", "context"),
        P(None, "dp", "context"),
        P(None, "dp", "context"),
        P(None, "dp", "context"),
        P("dp", None),
        P("dp", None),
        P("dp", None),
        P("dp", None),
    )
    return jax.shard_map(
        per_device, mesh=mesh, in_specs=in_specs, out_specs=out_specs, check_vma=False
    )
```

profile of v0, /device:TPU:6, one launch (start us, length us, event | category | flops | bytes accessed | tf_op | source)
XLA Modules:
  0.0 1538.8 jit_solution(13658399015251073395)
XLA Ops:
  8.4 6.0 multiply_reduce_fusion.5
  15.3 1.8 copy.197
  17.1 21.2 %all-to-all-start = ((f32[1536,1,128]{0,1,2:T(1,128)}), f32[1536,1,128]{0,1,2:T(1,128)S(1)}, u32[]{:S(2)}, u32[]{:S(2)}) async-start(f32[1536,1,128]{0,1,2:T(1,128)} %copy.197), calls=%async_computation | async-start | bytes 1572864 | tf_op jit(solution)/shard_map/all_to_all | solution.py:100
  38.4 40.0 %all-to-all-done = f32[1536,1,128]{0,1,2:T(1,128)S(1)} async-done(((f32[1536,1,128]{0,1,2:T(1,128)}), f32[1536,1,128]{0,1,2:T(1,128)S(1)}, u32[]{:S(2)}, u32[]{:S(2)}) %all-to-all-start) | async-done | bytes 786464 | tf_op jit(solution)/shard_map/all_to_all | solution.py:100
  78.4 1.9 reduce
  80.8 2.7 fusion.18
  83.5 3.9 multiply_add_fusion.1
  87.4 3.7 copy.200
  91.1 23.5 %all-to-all-start.1 = ((f32[1536,2,128]{0,1,2:T(2,128)}), f32[1536,2,128]{0,1,2:T(2,128)S(1)}, u32[]{:S(2)}, u32[]{:S(2)}) async-start(f32[1536,2,128]{0,1,2:T(2,128)} %copy.200), calls=%async_computation.1 | async-start | bytes 3145728 | tf_op jit(solution)/shard_map/all_to_all | solution.py:104
  114.6 2.2 copy.203
  116.8 33.1 %all-to-all-done.1 = f32[1536,2,128]{0,1,2:T(2,128)S(1)} async-done(((f32[1536,2,128]{0,1,2:T(2,128)}), f32[1536,2,128]{0,1,2:T(2,128)S(1)}, u32[]{:S(2)}, u32[]{:S(2)}) %all-to-all-start.1) | async-done | bytes 1572896 | tf_op jit(solution)/shard_map/all_to_all | solution.py:104
  149.9 48.3 %all-to-all-start.2 = ((f32[1536,2,128]{0,1,2:T(2,128)}), f32[1536,2,128]{0,1,2:T(2,128)S(1)}, u32[]{:S(2)}, u32[]{:S(2)}) async-start(f32[1536,2,128]{0,1,2:T(2,128)} %copy.203), calls=%async_computation.2 | async-start | bytes 3145728 | tf_op jit(solution)/shard_map/all_to_all | solution.py:105
  198.2 2.0 copy.201
  200.2 2.5 copy.202
  202.7 2.8 fusion.49
  205.5 32.2 %all-to-all-done.2 = f32[1536,2,128]{0,1,2:T(2,128)S(1)} async-done(((f32[1536,2,128]{0,1,2:T(2,128)}), f32[1536,2,128]{0,1,2:T(2,128)S(1)}, u32[]{:S(2)}, u32[]{:S(2)}) %all-to-all-start.2) | async-done | bytes 1572896 | tf_op jit(solution)/shard_map/all_to_all | solution.py:105
  237.7 2.0 copy.204
  239.7 2.5 copy.205
  254.1 11.2 all-to-all-start.3
  266.6 21.2 %all-to-all-done.3 = f32[1024,2,128]{0,1,2:T(2,128)S(1)} async-done(((f32[1024,2,128]{0,1,2:T(2,128)}), f32[1024,2,128]{0,1,2:T(2,128)S(1)}, u32[]{:S(2)}, u32[]{:S(2)}) %all-to-all-start.3) | async-done | bytes 1048608 | tf_op jit(solution)/shard_map/all_to_all | solution.py:125
  287.8 9.1 all-to-all-start.4
  298.5 49.5 %all-to-all-done.4 = f32[1024,2,128]{0,1,2:T(2,128)S(1)} async-done(((f32[1024,2,128]{0,1,2:T(2,128)}), f32[1024,2,128]{0,1,2:T(2,128)S(1)}, u32[]{:S(2)}, u32[]{:S(2)}) %all-to-all-start.4) | async-done | bytes 1048608 | tf_op jit(solution)/shard_map/all_to_all | solution.py:126
  350.9 8.1 all-to-all-start.5
  359.4 40.1 %all-to-all-done.5 = f32[1024,64,2]{0,2,1:T(2,128)S(1)} async-done(((f32[1024,64,2]{0,2,1:T(2,128)}), f32[1024,64,2]{0,2,1:T(2,128)S(1)}, u32[]{:S(2)}, u32[]{:S(2)}) %all-to-all-start.5) | async-done | bytes 524320 | tf_op jit(solution)/shard_map/all_to_all | solution.py:129
  401.1 8.1 multiply_reduce_fusion
  409.9 31.7 %all_to_all.186 = f32[1536,1,128]{0,1,2:T(1,128)S(1)} all-to-all(f32[1536,1,128]{0,1,2:T(1,128)S(1)} %copy.218), channel_id=1, replica_groups=mesh['dp'=8,'context'=64] {'context'}, dimensions={2} | all-to-all | bytes 1572864 | tf_op jit(solution)/shard_map/all_to_all | solution.py:100
  441.6 1.9 reduce.1
  443.9 2.7 fusion.15
  446.6 3.9 multiply_add_fusion
  450.5 3.7 copy.221
  454.2 9.4 all-to-all-start.7
  463.6 2.2 copy.224
  465.8 23.4 %all-to-all-done.7 = f32[1536,2,128]{0,1,2:T(2,128)S(1)} async-done(((f32[1536,2,128]{0,1,2:T(2,128)}), f32[1536,2,128]{0,1,2:T(2,128)S(1)}, u32[]{:S(2)}, u32[]{:S(2)}) %all-to-all-start.7) | async-done | bytes 1572896 | tf_op jit(solution)/shard_map/all_to_all | solution.py:104
  489.2 8.9 all-to-all-start.8
  498.1 2.0 copy.222
  500.0 2.5 copy.223
  502.5 2.8 fusion.43
  505.3 58.6 %all-to-all-done.8 = f32[1536,2,128]{0,1,2:T(2,128)S(1)} async-done(((f32[1536,2,128]{0,1,2:T(2,128)}), f32[1536,2,128]{0,1,2:T(2,128)S(1)}, u32[]{:S(2)}, u32[]{:S(2)}) %all-to-all-start.8) | async-done | bytes 1572896 | tf_op jit(solution)/shard_map/all_to_all | solution.py:105
  564.0 2.0 copy.225
  566.0 2.7 copy.226
  580.5 12.2 all-to-all-start.9
  594.1 33.6 %all-to-all-done.9 = f32[1024,2,128]{0,1,2:T(2,128)S(1)} async-done(((f32[1024,2,128]{0,1,2:T(2,128)}), f32[1024,2,128]{0,1,2:T(2,128)S(1)}, u32[]{:S(2)}, u32[]{:S(2)}) %all-to-all-start.9) | async-done | bytes 1048608 | tf_op jit(solution)/shard_map/all_to_all | solution.py:125
  627.7 12.6 all-to-all-start.10
  641.9 37.3 %all-to-all-done.10 = f32[1024,2,128]{0,1,2:T(2,128)S(1)} async-done(((f32[1024,2,128]{0,1,2:T(2,128)}), f32[1024,2,128]{0,1,2:T(2,128)S(1)}, u32[]{:S(2)}, u32[]{:S(2)}) %all-to-all-start.10) | async-done | bytes 1048608 | tf_op jit(solution)/shard_map/all_to_all | solution.py:126
  682.0 9.7 all-to-all-start.11
  692.7 22.0 %all-to-all-done.11 = f32[1024,64,2]{0,2,1:T(2,128)S(1)} async-done(((f32[1024,64,2]{0,2,1:T(2,128)}), f32[1024,64,2]{0,2,1:T(2,128)S(1)}, u32[]{:S(2)}, u32[]{:S(2)}) %all-to-all-start.11) | async-done | bytes 524320 | tf_op jit(solution)/shard_map/all_to_all | solution.py:129
  715.1 4.8 multiply_reduce_fusion.2
  721.9 806.8 %all-reduce.3.cloned.1.call-done = (f32[512,16]{0,1:T(8,128)}, f32[512,16]{0,1:T(8,128)}, f32[512,16]{0,1:T(8,128)}, f32[512,16]{0,1:T(8,128)}) async-done(((f32[512,16]{0,1:T(8,128)}, f32[512,16]{0,1:T(8,128)}, f32[512,16]{0,1:T(8,128)}, f32[512,16]{0,1:T(8,128)}), (f32[512,16]{0,1:T(8,128)}, f32[512,16]{0,1:T(8,128)}, f32[512,16]{0,1:T(8,128)}, f32[512,16]{0,1:T(8,128)})) %all-reduce.3.cloned.1.call-update) | async-done | bytes 131088 | tf_op jit(solution)/shard_map/psum | solution.py:183
  (123 shorter events, 46.5 us)
Async XLA Ops:
  7.2 7.2 copy-start.20
  7.2 7.2 copy-start.19
  7.2 7.2 copy-start.18
  8.2 7.0 copy-start.13
  8.2 6.9 copy-start.2
  8.2 6.9 copy-start.3
  8.3 6.9 copy-start.4
  8.4 6.8 copy-start.15
  17.1 61.4 %all-to-all-start = ((f32[1536,1,128]{0,1,2:T(1,128)}), f32[1536,1,128]{0,1,2:T(1,128)S(1)}, u32[]{:S(2)}, u32[]{:S(2)}) async-start(f32[1536,1,128]{0,1,2:T(1,128)} %copy.197), calls=%async_computation | async-start | bytes 1572864 | tf_op jit(solution)/shard_map/all_to_all | solution.py:100
  91.1 58.8 %all-to-all-start.1 = ((f32[1536,2,128]{0,1,2:T(2,128)}), f32[1536,2,128]{0,1,2:T(2,128)S(1)}, u32[]{:S(2)}, u32[]{:S(2)}) async-start(f32[1536,2,128]{0,1,2:T(2,128)} %copy.200), calls=%async_computation.1 | async-start | bytes 3145728 | tf_op jit(solution)/shard_map/all_to_all | solution.py:104
  149.9 87.8 %all-to-all-start.2 = ((f32[1536,2,128]{0,1,2:T(2,128)}), f32[1536,2,128]{0,1,2:T(2,128)S(1)}, u32[]{:S(2)}, u32[]{:S(2)}) async-start(f32[1536,2,128]{0,1,2:T(2,128)} %copy.203), calls=%async_computation.2 | async-start | bytes 3145728 | tf_op jit(solution)/shard_map/all_to_all | solution.py:105
  242.2 1.7 copy-start
  254.1 33.7 %all-to-all-start.3 = ((f32[1024,2,128]{0,1,2:T(2,128)}), f32[1024,2,128]{0,1,2:T(2,128)S(1)}, u32[]{:S(2)}, u32[]{:S(2)}) async-start(f32[1024,2,128]{0,1,2:T(2,128)} %copy.208), calls=%async_computation.3 | async-start | bytes 2097152 | tf_op jit(solution)/shard_map/all_to_all | solution.py:125
  287.8 60.2 %all-to-all-start.4 = ((f32[1024,2,128]{0,1,2:T(2,128)}), f32[1024,2,128]{0,1,2:T(2,128)S(1)}, u32[]{:S(2)}, u32[]{:S(2)}) async-start(f32[1024,2,128]{0,1,2:T(2,128)} %copy.211), calls=%async_computation.4 | async-start | bytes 2097152 | tf_op jit(solution)/shard_map/all_to_all | solution.py:126
  349.7 9.4 copy-start.23
  349.7 9.4 copy-start.25
  349.7 9.7 copy-start.5
  349.7 9.7 copy-start.7
  350.9 48.7 %all-to-all-start.5 = ((f32[1024,64,2]{0,2,1:T(2,128)}), f32[1024,64,2]{0,2,1:T(2,128)S(1)}, u32[]{:S(2)}, u32[]{:S(2)}) async-start(f32[1024,64,2]{0,2,1:T(2,128)} %copy.214), calls=%async_computation.5 | async-start | bytes 1048576 | tf_op jit(solution)/shard_map/all_to_all | solution.py:129
  359.2 41.8 %copy-start.9 = (f32[512,16]{1,0:T(8,128)}, f32[512,16]{1,0:T(8,128)S(1)}, u32[]{:S(2)}) copy-start(f32[512,16]{1,0:T(8,128)S(1)} %copy.216) | copy-start | bytes 98308
  359.4 41.7 %copy-start.11 = (f32[512,16]{1,0:T(8,128)}, f32[512,16]{1,0:T(8,128)S(1)}, u32[]{:S(2)}) copy-start(f32[512,16]{1,0:T(8,128)S(1)} %copy.217) | copy-start | bytes 98308
  399.6 1.5 copy-start.14
  399.6 1.5 copy-start.16
  454.2 35.0 %all-to-all-start.7 = ((f32[1536,2,128]{0,1,2:T(2,128)}), f32[1536,2,128]{0,1,2:T(2,128)S(1)}, u32[]{:S(2)}, u32[]{:S(2)}) async-start(f32[1536,2,128]{0,1,2:T(2,128)} %copy.221), calls=%async_computation.7 | async-start | bytes 3145728 | tf_op jit(solution)/shard_map/all_to_all | solution.py:104
  489.2 74.8 %all-to-all-start.8 = ((f32[1536,2,128]{0,1,2:T(2,128)}), f32[1536,2,128]{0,1,2:T(2,128)S(1)}, u32[]{:S(2)}, u32[]{:S(2)}) async-start(f32[1536,2,128]{0,1,2:T(2,128)} %copy.224), calls=%async_computation.8 | async-start | bytes 3145728 | tf_op jit(solution)/shard_map/all_to_all | solution.py:105
  568.7 1.7 copy-start.1
  580.5 47.1 %all-to-all-start.9 = ((f32[1024,2,128]{0,1,2:T(2,128)}), f32[1024,2,128]{0,1,2:T(2,128)S(1)}, u32[]{:S(2)}, u32[]{:S(2)}) async-start(f32[1024,2,128]{0,1,2:T(2,128)} %copy.229), calls=%async_computation.9 | async-start | bytes 2097152 | tf_op jit(solution)/shard_map/all_to_all | solution.py:125
  627.7 51.5 %all-to-all-start.10 = ((f32[1024,2,128]{0,1,2:T(2,128)}), f32[1024,2,128]{0,1,2:T(2,128)S(1)}, u32[]{:S(2)}, u32[]{:S(2)}) async-start(f32[1024,2,128]{0,1,2:T(2,128)} %copy.232), calls=%async_computation.10 | async-start | bytes 2097152 | tf_op jit(solution)/shard_map/all_to_all | solution.py:126
  680.8 11.0 copy-start.17
  680.8 11.2 copy-start.21
  680.8 11.2 copy-start.22
  682.0 32.6 %all-to-all-start.11 = ((f32[1024,64,2]{0,2,1:T(2,128)}), f32[1024,64,2]{0,2,1:T(2,128)S(1)}, u32[]{:S(2)}, u32[]{:S(2)}) async-start(f32[1024,64,2]{0,2,1:T(2,128)} %copy.235), calls=%async_computation.11 | async-start | bytes 1048576 | tf_op jit(solution)/shard_map/all_to_all | solution.py:129
  691.7 23.3 %copy-start.10 = (f32[512,16]{1,0:T(8,128)S(1)}, f32[512,16]{1,0:T(8,128)}, u32[]{:S(2)}) copy-start(f32[512,16]{1,0:T(8,128)} %copy-done.9) | copy-start | bytes 98308
  691.7 23.3 %copy-start.12 = (f32[512,16]{1,0:T(8,128)S(1)}, f32[512,16]{1,0:T(8,128)}, u32[]{:S(2)}) copy-start(f32[512,16]{1,0:T(8,128)} %copy-done.11) | copy-start | bytes 98308
  691.8 837.0 %all-reduce.3.cloned.1.call-start = ((), (), s32[]{:S(2)}) async-start(), calls=%async_computation.12 | async-start | bytes 262144 | tf_op jit(solution)/shard_map/psum | solution.py:183
  715.1 5.4 copy-start.24
  715.1 5.4 copy-start.26
  715.1 6.1 copy-start.6
  715.1 6.1 copy-start.8
Sparse Core Ops, SparseCore 0:
  721.3 807.3 all-reduce.2
where the time goes:
time: 1550 us; the launch traced here: 1540 us
  waiting for transfers between devices  1200 us (77%)
  starting transfers between devices  174 us (11%)
  local copies, waits for them, and re-layouts  45.6 us (3%)
  matrix products  43.3 us (3%)
  blocking collectives  31.7 us (2%)
  other arithmetic  30.7 us (2%)
    psum x1, waiting for transfers between devices, per_device(): summed = lax.psum((res_one, log_one, res_two, log_two), 'context')  807 us
    all_to_all x2, waiting for transfers between devices, forward(): lax.all_to_all(spread[1], 'context', split_axis=2, concat_axis=1, tiled=T...  90.9 us
    all_to_all x2, waiting for transfers between devices, inverse(): lax.all_to_all(twisted_imag, 'context', split_axis=2, concat_axis=1, tile...  86.9 us
    all_to_all x2, waiting for transfers between devices, inverse(): lax.all_to_all(mixed, 'context', split_axis=1, concat_axis=2, tiled=True)  62.1 us
    all_to_all x2, starting transfers between devices, forward(): lax.all_to_all(spread[1], 'context', split_axis=2, concat_axis=1, tiled=T...  57.2 us
    all_to_all x2, waiting for transfers between devices, forward(): lax.all_to_all(spread[0], 'context', split_axis=2, concat_axis=1, tiled=T...  56.5 us
    all_to_all x2, waiting for transfers between devices, inverse(): lax.all_to_all(twisted_real, 'context', split_axis=2, concat_axis=1, tile...  54.8 us
    dot_general x24, matrix products, matmul(): jnp.einsum(form, left, right, precision=lax.Precision.HIGHEST, preferred_...  43.3 us
  transfers between devices with their start and end apart: 12, of which 12 were waited for; matrix products, arithmetic and copies ran while one was open for 2% of the time, Pallas kernels for 0%

commit v1 on v0

v1 whole, which is shorter than its diff:
```python
import math

import jax
import jax.numpy as jnp
from jax import lax
from jax.experimental import pallas as pl
from jax.experimental.pallas import tpu as pltpu
from jax.sharding import PartitionSpec as P

MESH = pl.DeviceIdType.MESH
LOCAL = 128
CHAN = 512
ORDER = 16
STATE = (8, 8, 128)
SCALE = 1.0 / math.sqrt(8192.0)
UNROLL = 4

(AMP1, RATE1, AMP2, RATE2, S2, M2, L02, L12, ZA1, ZB1, ZA2, ZB2, C2, S1, EU, EN, EN1, EN2) = range(18)


def wait_bytes(ref, sem):
    pltpu.make_async_copy(ref, ref, sem).wait()


def kernel(
    value, key_one, gate_one, conv_one, key_two, gate_two, grad_out, res1, lr1, res2, lr2,
    back1_out, back2_out, sums_out,
    wide, narrow, in_sem, src2_t, gain_t, sig1_t, sig2_t, src1_t, back2_t, back1_t, par,
    keep, usend, urecv, nsend, nrecv, vsend, vrecv, grads, rs_recv, zred, piece,
    us_sem, ur_sem, ns_sem, nr_sem, vs_sem, vr_sem, p_send, p_recv,
):
    dp = lax.axis_index("dp")
    ctx = lax.axis_index("context")
    y, x, z = ctx // 16, (ctx // 4) % 4, ctx % 4
    me = ctx // 4
    coords = (y, x, z)

    def at(axis, d):
        if axis == 0:
            return (dp, ((y + d) % 4) * 16 + x * 4 + z)
        if axis == 1:
            return (dp, y * 16 + ((x + d) % 4) * 4 + z)
        return (dp, y * 16 + x * 4 + (z + d) % 4)

    plane = [
        (((y + e) % 4) * 4 + (x + f) % 4) for e in range(4) for f in range(4) if e or f
    ]

    barrier = pltpu.get_barrier_semaphore()
    for q in plane:
        pl.semaphore_signal(barrier, inc=1, device_id=(dp, q * 4 + z), device_id_type=MESH)
    for d in (1, 2, 3):
        pl.semaphore_signal(barrier, inc=1, device_id=at(2, d), device_id_type=MESH)

    wide_in = (grad_out, gate_two, key_two, gate_one, conv_one, key_one, value)
    narrow_in = (lr2, lr1, res2, res1)
    loads = []
    for i, ref in enumerate(narrow_in):
        loads.append(pltpu.make_async_copy(ref, narrow.at[i], in_sem.at[7 + i]))
    for i, ref in enumerate(wide_in):
        loads.append(pltpu.make_async_copy(ref.at[0], wide.at[i], in_sem.at[i]))
    for load in loads:
        load.start()

    for i in range(4):
        loads[i].wait()
        for c in range(4):
            par[i, pl.ds(c, ORDER, stride=4), :] = narrow[i, c * 128 : (c + 1) * 128, :].T
    rate2 = jnp.exp(par[0]).reshape(STATE)
    rate1 = jnp.exp(par[1]).reshape(STATE)
    keep[RATE2] = rate2
    keep[RATE1] = rate1
    keep[AMP2] = par[2].reshape(STATE) * jnp.sqrt(2.0 * rate2)
    keep[AMP1] = par[3].reshape(STATE) * jnp.sqrt(2.0 * rate1)

    def block(i, c):
        return wide[i, c * 128 : (c + 1) * 128, :].astype(jnp.float32)

    def put(ref, c, tile):
        flipped = tile.T
        ref[pl.ds(c, LOCAL, stride=8), :] = flipped
        ref[pl.ds(c + 4, LOCAL, stride=8), :] = flipped

    def row(ref, t):
        return ref[pl.ds(pl.multiple_of(t * 8, 8), 8), :][None]

    zero = jnp.zeros(STATE, jnp.float32)

    loads[4].wait()
    loads[5].wait()
    for c in range(4):
        put(src2_t, c, block(0, c) * block(1, c))

    decay2 = jnp.exp(-rate2)

    def first(i, state):
        return decay2 * state + row(src2_t, LOCAL - 1 - i)

    state = lax.fori_loop(0, LOCAL, first, zero, unroll=UNROLL)
    keep[S2] = state
    usend[0, 0] = state

    for i in range(6, 11):
        loads[i].wait()
    for c in range(4):
        kt, go = block(2, c), block(3, c)
        put(gain_t, c, kt * go)
        put(sig2_t, c, kt * (go * block(4, c)))
        put(sig1_t, c, block(5, c) * block(6, c))

    decay1 = jnp.exp(-keep[RATE1])

    def ahead(t, st):
        a0, a1, b0, b1 = st
        u = a0 + row(sig1_t, t)
        v = b0 + row(sig2_t, t)
        return decay1 * u, decay1 * (a1 + u), decay2 * v, decay2 * (b1 + v)

    za1, zb1, za2, zb2 = lax.fori_loop(0, LOCAL, ahead, (zero,) * 4, unroll=UNROLL)
    keep[ZA1], keep[ZB1], keep[ZA2], keep[ZB2] = za1, zb1, za2, zb2
    nsend[0, 0, 0], nsend[0, 0, 1], nsend[0, 0, 2] = za1, zb1, za2

    pl.semaphore_wait(barrier, 18)

    def send(axis, buf, recv, ssem, rsem, suffix):
        for d in (1, 2, 3):
            which = 0 if axis == 0 else (coords[axis] + d) // 4
            pltpu.make_async_remote_copy(
                src_ref=buf.at[axis, which],
                dst_ref=recv.at[axis, 3 - d if suffix else d - 1],
                send_sem=ssem.at[axis],
                recv_sem=rsem.at[axis],
                device_id=at(axis, d),
                device_id_type=MESH,
            ).start()

    strides = (2048.0, 512.0, 128.0)

    def masked(axis, array, d, suffix):
        if axis:
            return array
        there = (y + d < 4) if suffix else (y >= d)
        return jnp.where(there, array, 0.0)

    def suffix_merge(axis, recv, rsem, far, rate):
        wait_bytes(recv.at[axis], rsem.at[axis])
        power = jnp.exp(-strides[axis] * rate)
        for d in (3, 2, 1):
            far = masked(axis, recv[axis, d - 1], d, True) + power * far
        return far, power

    def prefix_merge(axis):
        wait_bytes(nrecv.at[axis], nr_sem.at[axis])
        step = strides[axis]
        p1 = jnp.exp(-step * keep[RATE1])
        p2 = jnp.exp(-step * keep[RATE2])
        if axis == 0:
            f0, f1, f2 = zero, zero, zero
        else:
            f0, f1, f2 = keep[EN], keep[EN1], keep[EN2]
        for d in (3, 2, 1):
            f1 = masked(axis, nrecv[axis, d - 1, 1], d, False) + p1 * (f1 + step * f0)
            f0 = masked(axis, nrecv[axis, d - 1, 0], d, False) + p1 * f0
            f2 = masked(axis, nrecv[axis, d - 1, 2], d, False) + p2 * f2
        keep[EN], keep[EN1], keep[EN2] = f0, f1, f2
        if axis < 2:
            nsend[axis + 1, 1, 0], nsend[axis + 1, 1, 1], nsend[axis + 1, 1, 2] = f0, f1, f2
            nsend[axis + 1, 0, 0] = keep[ZA1] + p1 * f0
            nsend[axis + 1, 0, 1] = keep[ZB1] + p1 * (f1 + step * f0)
            nsend[axis + 1, 0, 2] = keep[ZA2] + p2 * f2

    def back_step(axis, buf, recv, ssem, rsem, own, rate):
        far = zero if axis == 0 else keep[EU]
        far, power = suffix_merge(axis, recv, rsem, far, keep[rate])
        keep[EU] = far
        if axis < 2:
            buf[axis + 1, 0] = far
            buf[axis + 1, 1] = keep[own] + power * far
            send(axis + 1, buf, recv, ssem, rsem, True)
        return far

    send(0, usend, urecv, us_sem, ur_sem, True)
    send(0, nsend, nrecv, ns_sem, nr_sem, False)

    def near(src_t, sig_t, decay):
        def body(i, st):
            t = LOCAL - 1 - i
            x0, x1, l0, l1 = st
            x1 = decay * (x1 + x0)
            x0 = decay * x0 + row(src_t, t)
            sig = row(sig_t, t)
            return x0, x1, l0 + sig * x0, l1 + sig * x1

        return lax.fori_loop(0, LOCAL, body, (zero,) * 4, unroll=UNROLL)

    unused, m2, l02, l12 = near(src2_t, sig2_t, decay2)
    keep[M2], keep[L02], keep[L12] = m2, l02, l12

    back_step(0, usend, urecv, us_sem, ur_sem, S2, RATE2)
    prefix_merge(0)
    send(1, nsend, nrecv, ns_sem, nr_sem, False)
    back_step(1, usend, urecv, us_sem, ur_sem, S2, RATE2)
    prefix_merge(1)
    send(2, nsend, nrecv, ns_sem, nr_sem, False)
    c2 = back_step(2, usend, urecv, us_sem, ur_sem, S2, RATE2)
    keep[C2] = c2

    decay1 = jnp.exp(-keep[RATE1])
    decay2 = jnp.exp(-keep[RATE2])
    amp2 = keep[AMP2]

    def middle(i, st):
        t = LOCAL - 1 - i
        xa, xb = st
        xa = decay2 * xa + row(src2_t, t)
        part = jnp.sum(amp2 * xa, axis=0)
        back = part + pltpu.roll(part, 4, 0)
        here = pl.ds(pl.multiple_of(t * 8, 8), 8)
        back2_t[here, :] = back
        source = back * gain_t[here, :]
        src1_t[here, :] = source
        return xa, decay1 * xb + source[None]

    unused, s1 = lax.fori_loop(0, LOCAL, middle, (c2, zero), unroll=UNROLL)
    keep[S1] = s1
    vsend[0, 0] = s1
    send(0, vsend, vrecv, vs_sem, vr_sem, True)

    unused, m1, l01, l11 = near(src1_t, sig1_t, decay1)
    prefix_merge(2)
    y1, y11, y2 = keep[EN], keep[EN1], keep[EN2]
    rate1, amp1 = keep[RATE1], keep[AMP1]
    zero_sum = l01 + s1 * y1
    one_sum = l11 + s1 * y11 + m1 * y1
    grads[0] = zero_sum * jnp.sqrt(2.0 * rate1) * SCALE
    grads[1] = amp1 * (0.5 * zero_sum - rate1 * one_sum) * SCALE
    rate2, amp2 = keep[RATE2], keep[AMP2]
    c2 = keep[C2]
    zero_sum = keep[L02] + keep[ZA2] * c2
    one_sum = keep[L12] + keep[ZB2] * c2 + keep[M2] * y2 + (128.0 * jnp.exp(-128.0 * rate2)) * (y2 * c2)
    grads[2] = zero_sum * jnp.sqrt(2.0 * rate2) * SCALE
    grads[3] = amp2 * (0.5 * zero_sum - rate2 * one_sum) * SCALE

    def share(ref, q):
        return ref.at[q // 4, pl.ds((q % 4) * 2, 2)]

    for i, q in enumerate(plane):
        pltpu.make_async_remote_copy(
            src_ref=share(grads, q), dst_ref=rs_recv.at[i], send_sem=p_send.at[0], recv_sem=p_recv.at[0],
            device_id=(dp, q * 4 + z), device_id_type=MESH,
        ).start()

    back_step(0, vsend, vrecv, vs_sem, vr_sem, S1, RATE1)

    wait_bytes(rs_recv, p_recv.at[0])
    total = grads[me // 4, pl.ds((me % 4) * 2, 2)]
    for i in range(15):
        total = total + rs_recv[i]
    zred[z] = total
    for d in (1, 2, 3):
        pltpu.make_async_remote_copy(
            src_ref=zred.at[z], dst_ref=zred.at[z], send_sem=p_send.at[1], recv_sem=p_recv.at[1],
            device_id=at(2, d), device_id_type=MESH,
        ).start()

    back_step(1, vsend, vrecv, vs_sem, vr_sem, S1, RATE1)

    for c in range(4):
        back2_out[c * 128 : (c + 1) * 128, :] = back2_t[pl.ds(c, LOCAL, stride=8), :].T

    wait_bytes(zred.at[pl.ds(0, 3)], p_recv.at[1])
    total = (zred[0] + zred[1]) + (zred[2] + zred[3])
    piece[...] = total
    sums_out[me] = total
    for i, q in enumerate(plane):
        pltpu.make_async_remote_copy(
            src_ref=piece, dst_ref=sums_out.at[me], send_sem=p_send.at[2], recv_sem=p_recv.at[2],
            device_id=(dp, q * 4 + z), device_id_type=MESH,
        ).start()

    c1 = back_step(2, vsend, vrecv, vs_sem, vr_sem, S1, RATE1)
    decay1 = jnp.exp(-keep[RATE1])
    amp1 = keep[AMP1]

    def last(i, xa):
        t = LOCAL - 1 - i
        xa = decay1 * xa + row(src1_t, t)
        part = jnp.sum(amp1 * xa, axis=0)
        back1_t[pl.ds(pl.multiple_of(t * 8, 8), 8), :] = part + pltpu.roll(part, 4, 0)
        return xa

    lax.fori_loop(0, LOCAL, last, c1, unroll=UNROLL)
    for c in range(4):
        back1_out[c * 128 : (c + 1) * 128, :] = back1_t[pl.ds(c, LOCAL, stride=8), :].T

    for axis in range(3):
        wait_bytes(urecv.at[axis], us_sem.at[axis])
        wait_bytes(nrecv.at[axis], ns_sem.at[axis])
        wait_bytes(vrecv.at[axis], vs_sem.at[axis])
    wait_bytes(rs_recv, p_send.at[0])
    wait_bytes(zred.at[pl.ds(0, 3)], p_send.at[1])
    wait_bytes(rs_recv, p_send.at[2])
    wait_bytes(sums_out.at[pl.ds(0, 15)], p_recv.at[2])


def per_device(
    value, key_one, gate_one, conv_one, key_two, gate_two, conv_two, grad_out,
    residues_one, log_rate_one, residues_two, log_rate_two,
):
    f32 = jnp.float32
    vmem = pltpu.VMEM
    dma = pltpu.SemaphoreType.DMA
    turned = vmem((LOCAL * 8, 128), f32)
    back_one, back_two, sums = pl.pallas_call(
        kernel,
        out_shape=[
            jax.ShapeDtypeStruct((CHAN, LOCAL), f32),
            jax.ShapeDtypeStruct((CHAN, LOCAL), f32),
            jax.ShapeDtypeStruct((16, 2, 8, 128), f32),
        ],
        in_specs=[pl.BlockSpec(memory_space=pl.ANY)] * 11,
        out_specs=[pl.BlockSpec(memory_space=pltpu.VMEM)] * 3,
        scratch_shapes=[
            vmem((7, CHAN, LOCAL), jnp.bfloat16),
            vmem((4, CHAN, ORDER), f32),
            dma((11,)),
            turned, turned, turned, turned, turned, turned, turned,
            vmem((4, 64, 128), f32),
            vmem((18,) + STATE, f32),
            vmem((3, 2) + STATE, f32),
            vmem((3, 3) + STATE, f32),
            vmem((3, 2, 3) + STATE, f32),
            vmem((3, 3, 3) + STATE, f32),
            vmem((3, 2) + STATE, f32),
            vmem((3, 3) + STATE, f32),
            vmem((4,) + STATE, f32),
            vmem((15, 2, 8, 128), f32),
            vmem((4, 2, 8, 128), f32),
            vmem((2, 8, 128), f32),
            dma((3,)), dma((3,)), dma((3,)), dma((3,)), dma((3,)), dma((3,)), dma((3,)), dma((3,)),
        ],
        compiler_params=pltpu.CompilerParams(
            collective_id=0, has_side_effects=True, vmem_limit_bytes=32 * 1024 * 1024
        ),
        name="hyena_back",
    )(
        value, key_one, gate_one, conv_one, key_two, gate_two, grad_out,
        residues_one, log_rate_one, residues_two, log_rate_two,
    )

    def widen(array):
        return array.astype(f32)

    def rounded(array):
        return array.astype(jnp.bfloat16)

    back_one, back_two = back_one[None], back_two[None]
    grad_gate_two = rounded(widen(grad_out) * widen(conv_two))
    grad_key_two = rounded(back_two * (widen(gate_one) * widen(conv_one)))
    grad_gate_one = rounded(back_two * widen(key_two) * widen(conv_one))
    grad_key_one = rounded(back_one * widen(value))
    grad_value = rounded(back_one * widen(key_one))
    grads = sums.reshape(4, ORDER, 4, 128).transpose(0, 2, 3, 1).reshape(4, CHAN, ORDER)
    return (
        grad_value, grad_key_one, grad_gate_one, grad_key_two, grad_gate_two,
        grads[0], grads[1], grads[2], grads[3],
    )


def solution(mesh):
    wide = P(None, "dp", "context")
    thin = P("dp", None)
    return jax.shard_map(
        per_device,
        mesh=mesh,
        in_specs=(wide,) * 8 + (thin,) * 4,
        out_specs=(wide,) * 5 + (thin,) * 4,
        check_vma=False,
    )
```

time: 1550 us -> 78.8 us (0.05)
  waiting for transfers between devices: 1200 us -> 0 us
  starting transfers between devices: 174 us -> 0 us
  Pallas kernels: 0 us -> 70.7 us
  matrix products: 43.3 us -> 0 us
  local copies, waits for them, and re-layouts: 45.6 us -> 4.66 us
  blocking collectives: 31.7 us -> 0 us
  other arithmetic: 30.7 us -> 1.57 us
    psum x1 -> x0, waiting for transfers between devices: 807 us -> none  [per_device(): summed = lax.psum((res_one, log_one, res_two, log_two), 'context')]
    all_to_all x11 -> x0, waiting for transfers between devices: 391 us -> none  [the longest x2 90.9 us: forward(): lax.all_to_all(spread[1], 'context', split_axis=2, concat_axis=1, tiled=T...]
    all_to_all x11 -> x0, starting transfers between devices: 174 us -> none  [the longest x2 57.2 us: forward(): lax.all_to_all(spread[1], 'context', split_axis=2, concat_axis=1, tiled=T...]
    pallas_call x0 -> x1, Pallas kernels: none -> 70.7 us  [per_device(): pl.pallas_call(kernel, out_shape=[jax.ShapeDtypeStruct((CHAN, LOCAL), f32...]
    dot_general x24 -> x0, matrix products: 43.3 us -> none  [matmul(): jnp.einsum(form, left, right, precision=lax.Precision.HIGHEST, preferred_...]
    all_to_all x1 -> x0, blocking collectives: 31.7 us -> none  [forward(): lax.all_to_all(block, 'context', split_axis=2, concat_axis=1, tiled=True)]
    all_to_all x14 -> x0, local copies, waits for them, and re-layouts: 21.2 us -> none  [the longest x4 9.19 us: forward(): lax.all_to_all(spread[1], 'context', split_axis=2, concat_axis=1, tiled=T...]
    reduce_sum x3 -> x0, other arithmetic: 18.9 us -> none  [the longest x2 13 us: local_filter(): decay = jnp.exp(-rate[:, :, None] * positions[None, None, :])]
  transfers between devices with their start and end apart: 12 -> 0, of which waited for: 12 -> 0; matrix products, arithmetic and copies ran while one was open for 2% -> 0% of each run, Pallas kernels for 0% -> 0%
where the time goes in v1:
time: 78.8 us; the launch traced here: 77.7 us
  Pallas kernels  70.7 us (90%)
  local copies, waits for them, and re-layouts  4.66 us (6%)
  other arithmetic  1.57 us (2%)
    pallas_call x1, Pallas kernels, per_device(): pl.pallas_call(kernel, out_shape=[jax.ShapeDtypeStruct((CHAN, LOCAL), f32...  70.7 us
    unnamed x26, local copies, waits for them, and re-layouts  3.39 us

profile of v1, /device:TPU:6, one launch (start us, length us, event | category | flops | bytes accessed | tf_op | source)
XLA Modules:
  0.0 77.7 jit_solution(7761199019480040774)
XLA Ops:
  0.6 0.0 copy-start.8
  0.7 0.0 copy-start.6
  0.7 0.9 %copy.21.res1 = f32[512,16]{1,0:T(8,128)S(1)} copy(f32[512,16]{0,1:T(8,128)} %param.20) | data formatting | bytes 65536 | tf_op args[8]
  1.6 0.0 copy-done.8
  1.6 0.0 copy-start.9
  1.6 0.0 copy-start.4
  1.6 0.0 copy-start.5
  1.6 0.1 copy.22.lr1
  1.8 0.6 copy-done.9
  2.4 0.0 copy-start.10
  2.4 0.0 copy-start.2
  2.4 0.0 copy-start.3
  2.4 0.1 copy.23.res2
  2.5 0.6 copy-done.10
  3.1 0.0 copy-start
  3.1 0.0 copy-start.1
  3.1 0.1 copy.24.lr2
  3.2 0.0 copy-done.6
  3.3 0.0 copy-done.4
  3.3 0.0 copy-done.5
  3.3 0.0 copy-done.2
  3.3 0.1 copy-done.3
  3.4 0.7 copy-done
  4.1 0.1 copy-done.1
  4.1 70.7 %hyena_back.1 = (f32[512,128]{1,0:T(8,128)S(1)}, f32[512,128]{1,0:T(8,128)S(1)}, f32[16,2,8,128]{3,2,1,0:T(8,128)S(1)}) custom-call(bf16[1,512,128]{2,1,0:T(8,128)(2,1)S(1)} %copy-done.2, bf16[1,512,128]{2,1,0:T(8,128)(2,1)S(1)} %copy-done.3, bf16[1,512,128]{2,1,0:T(8,128)(2,1)S(1)} %copy-done.4, bf16[1,512,128]{2,1,0:T(8,128)(2,1)S(1)} %copy-done.1, ...), custom_call_target="tpu_custom_call" | custom-call | tf_op jit(solution)/shard_map/hyena_back/pallas_call | solution.py:314
  74.8 0.6 copy_bitcast_fusion
  75.5 0.6 copy_bitcast_fusion.2
  76.1 0.0 copy-start.7
  76.1 0.9 %fusion.2 = (bf16[1,512,128]{2,1,0:T(8,128)(2,1)}, bf16[1,512,128]{2,1,0:T(8,128)(2,1)}, bf16[1,512,128]{2,1,0:T(8,128)(2,1)}, bf16[1,512,128]{2,1,0:T(8,128)(2,1)}) fusion(bf16[1,512,128]{2,1,0:T(8,128)(2,1)S(1)} %copy-done.1, f32[512,128]{1,0:T(8,128)S(1)} %get-tuple-element.13, bf16[1,512,128]{2,1,0:T(8,128)(2,1)S(1)} %copy-done.4, ...), kind=kLoop, calls=%fused_computation.4 | loop fusion | flops 983040 | bytes 1703936 | tf_op jit(solution)/shard_map/convert_element_type | solution.py:355
  77.0 0.0 copy-done.7
  77.0 0.7 multiply_convert_fusion
  (1 shorter events, 0.0 us)
Async XLA Ops:
  0.6 0.9 %copy-start.8 = (f32[512,16]{0,1:T(8,128)S(1)}, f32[512,16]{0,1:T(8,128)}, u32[]{:S(2)}) copy-start(f32[512,16]{0,1:T(8,128)} %param.21) | copy-start | bytes 98308
  0.7 2.6 %copy-start.6 = (bf16[1,512,128]{2,1,0:T(8,128)(2,1)S(1)}, bf16[1,512,128]{2,1,0:T(8,128)(2,1)}, u32[]{:S(2)}) copy-start(bf16[1,512,128]{2,1,0:T(8,128)(2,1)} %gate_two.1) | copy-start | bytes 393220
  1.6 0.8 copy-start.9
  1.6 1.7 %copy-start.4 = (bf16[1,512,128]{2,1,0:T(8,128)(2,1)S(1)}, bf16[1,512,128]{2,1,0:T(8,128)(2,1)}, u32[]{:S(2)}) copy-start(bf16[1,512,128]{2,1,0:T(8,128)(2,1)} %gate_one.1) | copy-start | bytes 393220
  1.6 1.6 %copy-start.5 = (bf16[1,512,128]{2,1,0:T(8,128)(2,1)S(1)}, bf16[1,512,128]{2,1,0:T(8,128)(2,1)}, u32[]{:S(2)}) copy-start(bf16[1,512,128]{2,1,0:T(8,128)(2,1)} %key_two.1) | copy-start | bytes 393220
  2.4 0.8 copy-start.10
  2.4 0.9 %copy-start.2 = (bf16[1,512,128]{2,1,0:T(8,128)(2,1)S(1)}, bf16[1,512,128]{2,1,0:T(8,128)(2,1)}, u32[]{:S(2)}) copy-start(bf16[1,512,128]{2,1,0:T(8,128)(2,1)} %value.1) | copy-start | bytes 393220
  2.4 1.0 %copy-start.3 = (bf16[1,512,128]{2,1,0:T(8,128)(2,1)S(1)}, bf16[1,512,128]{2,1,0:T(8,128)(2,1)}, u32[]{:S(2)}) copy-start(bf16[1,512,128]{2,1,0:T(8,128)(2,1)} %key_one.1) | copy-start | bytes 393220
  3.1 0.9 %copy-start = (bf16[1,512,128]{2,1,0:T(8,128)(2,1)S(1)}, bf16[1,512,128]{2,1,0:T(8,128)(2,1)}, u32[]{:S(2)}) copy-start(bf16[1,512,128]{2,1,0:T(8,128)(2,1)} %grad_out.1) | copy-start | bytes 393220
  3.1 1.0 %copy-start.1 = (bf16[1,512,128]{2,1,0:T(8,128)(2,1)S(1)}, bf16[1,512,128]{2,1,0:T(8,128)(2,1)}, u32[]{:S(2)}) copy-start(bf16[1,512,128]{2,1,0:T(8,128)(2,1)} %conv_one.1) | copy-start | bytes 393220
  76.1 0.9 %copy-start.7 = (bf16[1,512,128]{2,1,0:T(8,128)(2,1)S(1)}, bf16[1,512,128]{2,1,0:T(8,128)(2,1)}, u32[]{:S(2)}) copy-start(bf16[1,512,128]{2,1,0:T(8,128)(2,1)} %param.18) | copy-start | bytes 393220

commit v2 on v1

v2 whole, which is shorter than its diff:
```python
import math

import jax
import jax.numpy as jnp
from jax import lax
from jax.experimental import pallas as pl
from jax.experimental.pallas import tpu as pltpu
from jax.sharding import PartitionSpec as P

MESH = pl.DeviceIdType.MESH
LOCAL = 128
CHAN = 512
ORDER = 16
STATE = (8, 8, 128)
SCALE = 1.0 / math.sqrt(8192.0)
UNROLL = 4

(AMP1, RATE1, AMP2, RATE2, S2, M2, L02, L12, ZA2, ZB2, C2, S1, EU) = range(13)


def wait_bytes(ref, sem):
    pltpu.make_async_copy(ref, ref, sem).wait()


def kernel(
    value, key_one, gate_one, conv_one, key_two, gate_two, conv_two, grad_out, res1, lr1, res2, lr2,
    value_out, key1_out, gate1_out, key2_out, gate2_out, sums_out,
    wide, narrow, made, sums, in_sem, src2_t, gain_t, sig1_t, sig2_t, src1_t, back2_t, back1_t, par,
    keep, usend, urecv, nsend, nrecv, tsend, trecv, ysend, yrecv, vsend, vrecv, grads, rs_recv, zred, piece,
    us_sem, ur_sem, n_sem, ts_sem, tr_sem, vs_sem, vr_sem, p_send, p_recv, out_sem,
):
    dp = lax.axis_index("dp")
    ctx = lax.axis_index("context")
    y, x, z = ctx // 16, (ctx // 4) % 4, ctx % 4
    me = ctx // 4
    coords = (y, x, z)

    def at(axis, d):
        if axis == 0:
            return (dp, ((y + d) % 4) * 16 + x * 4 + z)
        if axis == 1:
            return (dp, y * 16 + ((x + d) % 4) * 4 + z)
        return (dp, y * 16 + x * 4 + (z + d) % 4)

    plane = [
        (((y + e) % 4) * 4 + (x + f) % 4) for e in range(4) for f in range(4) if e or f
    ]

    barrier = pltpu.get_barrier_semaphore()
    for q in plane:
        pl.semaphore_signal(barrier, inc=1, device_id=(dp, q * 4 + z), device_id_type=MESH)
    for d in (1, 2, 3):
        pl.semaphore_signal(barrier, inc=1, device_id=at(2, d), device_id_type=MESH)

    wide_in = (grad_out, gate_two, key_two, gate_one, conv_one, key_one, value, conv_two)
    narrow_in = (lr2, lr1, res2, res1)
    loads = []
    for i, ref in enumerate(narrow_in):
        loads.append(pltpu.make_async_copy(ref, narrow.at[i], in_sem.at[8 + i]))
    for i, ref in enumerate(wide_in):
        loads.append(pltpu.make_async_copy(ref.at[0], wide.at[i], in_sem.at[i]))
    for load in loads:
        load.start()

    for i in range(4):
        loads[i].wait()
        for c in range(4):
            par[i, pl.ds(c, ORDER, stride=4), :] = narrow[i, :, c * 128 : (c + 1) * 128]
    rate2 = jnp.exp(par[0]).reshape(STATE)
    rate1 = jnp.exp(par[1]).reshape(STATE)
    keep[RATE2] = rate2
    keep[RATE1] = rate1
    keep[AMP2] = par[2].reshape(STATE) * jnp.sqrt(2.0 * rate2)
    keep[AMP1] = par[3].reshape(STATE) * jnp.sqrt(2.0 * rate1)

    def block(i, c):
        return wide[i, c * 128 : (c + 1) * 128, :].astype(jnp.float32)

    def put(ref, c, tile):
        flipped = tile.T
        ref[pl.ds(c, LOCAL, stride=8), :] = flipped
        ref[pl.ds(c + 4, LOCAL, stride=8), :] = flipped

    def row(ref, t):
        return ref[pl.ds(pl.multiple_of(t * 8, 8), 8), :][None]

    zero = jnp.zeros(STATE, jnp.float32)

    loads[4].wait()
    loads[5].wait()
    for c in range(4):
        put(src2_t, c, block(0, c) * block(1, c))

    decay2 = jnp.exp(-rate2)

    def first(i, state):
        return decay2 * state + row(src2_t, LOCAL - 1 - i)

    state = lax.fori_loop(0, LOCAL, first, zero, unroll=UNROLL)
    keep[S2] = state
    usend[0, 0] = state

    for i in range(6, 12):
        loads[i].wait()
    for c in range(4):
        kt, go = block(2, c), block(3, c)
        put(gain_t, c, kt * go)
        put(sig2_t, c, kt * (go * block(4, c)))
        put(sig1_t, c, block(5, c) * block(6, c))

    decay1 = jnp.exp(-keep[RATE1])

    def ahead(t, st):
        a0, a1, b0, b1 = st
        u = a0 + row(sig1_t, t)
        v = b0 + row(sig2_t, t)
        return decay1 * u, decay1 * (a1 + u), decay2 * v, decay2 * (b1 + v)

    za1, zb1, za2, zb2 = lax.fori_loop(0, LOCAL, ahead, (zero,) * 4, unroll=UNROLL)
    keep[ZA2], keep[ZB2] = za2, zb2
    for k, array in enumerate((za1, zb1, za2)):
        nsend[:, k] = array.reshape(4, 2, 8, 128)

    pl.semaphore_wait(barrier, 18)

    def send(axis, buf, recv, ssem, rsem):
        for d in (1, 2, 3):
            which = 0 if axis == 0 else (coords[axis] + d) // 4
            pltpu.make_async_remote_copy(
                src_ref=buf.at[axis, which],
                dst_ref=recv.at[axis, 3 - d],
                send_sem=ssem.at[axis],
                recv_sem=rsem.at[axis],
                device_id=at(axis, d),
                device_id_type=MESH,
            ).start()

    strides = (2048.0, 512.0, 128.0)

    def masked(axis, array, d):
        return array if axis else jnp.where(y + d < 4, array, 0.0)

    def suffix_merge(axis, recv, rsem, far, rate):
        wait_bytes(recv.at[axis], rsem.at[axis])
        power = jnp.exp(-strides[axis] * rate)
        for d in (3, 2, 1):
            far = masked(axis, recv[axis, d - 1], d) + power * far
        return far, power

    def spread_signals():
        for d in (1, 2, 3):
            pltpu.make_async_remote_copy(
                src_ref=nsend.at[(z + d) % 4], dst_ref=nrecv.at[z], send_sem=n_sem.at[0], recv_sem=n_sem.at[1],
                device_id=at(2, d), device_id_type=MESH,
            ).start()
        nrecv[z] = nsend[z]

    def quarter_rates():
        return keep[RATE1, pl.ds(2 * z, 2)], keep[RATE2, pl.ds(2 * z, 2)]

    def shifted(state, length, powers):
        f0, f1, f2 = state
        return powers[0] * f0, powers[0] * (f1 + length * f0), powers[1] * f2

    def added(left, right):
        return tuple(p + q for p, q in zip(left, right))

    def line(i):
        return tuple(nrecv[i, k] for k in range(3))

    def total_lines():
        wait_bytes(nrecv.at[pl.ds(0, 3)], n_sem.at[1])
        powers = tuple(jnp.exp(-128.0 * rate) for rate in quarter_rates())
        state = line(0)
        for i in (1, 2, 3):
            state = added(line(i), shifted(state, 128.0, powers))
        for k in range(3):
            tsend[k] = state[k]
        for k in range(1, 16):
            @pl.when(me + k < 16)
            def _():
                pltpu.make_async_remote_copy(
                    src_ref=tsend, dst_ref=trecv.at[k - 1], send_sem=ts_sem.at[k - 1], recv_sem=tr_sem.at[k - 1],
                    device_id=(dp, (me + k) * 4 + z), device_id_type=MESH,
                ).start()


    def return_signals():
        near_powers = []
        powers = []
        for rate in quarter_rates():
            powers.append(jnp.exp(-512.0 * rate))
            near_powers.append(jnp.exp(-128.0 * rate))
        for k in range(1, 16):
            @pl.when(me >= k)
            def _():
                wait_bytes(trecv.at[k - 1], tr_sem.at[k - 1])
        state = tuple(jnp.zeros((2, 8, 128), jnp.float32) for _ in range(3))
        for k in range(15, 0, -1):
            there = me >= k
            block = tuple(jnp.where(there, trecv[k - 1, i], 0.0) for i in range(3))
            state = added(block, shifted(state, 512.0, powers))
        for i in range(4):
            for k in range(3):
                ysend[i, k] = state[k]
            state = added(line(i), shifted(state, 128.0, near_powers))
        for d in (1, 2, 3):
            pltpu.make_async_remote_copy(
                src_ref=ysend.at[(z + d) % 4], dst_ref=yrecv.at[z], send_sem=n_sem.at[2], recv_sem=n_sem.at[3],
                device_id=at(2, d), device_id_type=MESH,
            ).start()
        yrecv[z] = ysend[z]

    def back_step(axis, buf, recv, ssem, rsem, own, rate):
        far = zero if axis == 0 else keep[EU]
        far, power = suffix_merge(axis, recv, rsem, far, keep[rate])
        keep[EU] = far
        if axis < 2:
            buf[axis + 1, 0] = far
            buf[axis + 1, 1] = keep[own] + power * far
            send(axis + 1, buf, recv, ssem, rsem)
        return far

    send(0, usend, urecv, us_sem, ur_sem)
    spread_signals()

    def near(src_t, sig_t, decay):
        def body(i, st):
            t = LOCAL - 1 - i
            x0, x1, l0, l1 = st
            x1 = decay * (x1 + x0)
            x0 = decay * x0 + row(src_t, t)
            sig = row(sig_t, t)
            return x0, x1, l0 + sig * x0, l1 + sig * x1

        return lax.fori_loop(0, LOCAL, body, (zero,) * 4, unroll=UNROLL)

    unused, m2, l02, l12 = near(src2_t, sig2_t, decay2)
    keep[M2], keep[L02], keep[L12] = m2, l02, l12

    back_step(0, usend, urecv, us_sem, ur_sem, S2, RATE2)
    back_step(1, usend, urecv, us_sem, ur_sem, S2, RATE2)
    total_lines()
    return_signals()
    c2 = back_step(2, usend, urecv, us_sem, ur_sem, S2, RATE2)
    keep[C2] = c2

    decay1 = jnp.exp(-keep[RATE1])
    decay2 = jnp.exp(-keep[RATE2])
    amp2 = keep[AMP2]

    def middle(i, st):
        t = LOCAL - 1 - i
        xa, xb = st
        xa = decay2 * xa + row(src2_t, t)
        part = jnp.sum(amp2 * xa, axis=0)
        back = part + pltpu.roll(part, 4, 0)
        here = pl.ds(pl.multiple_of(t * 8, 8), 8)
        back2_t[here, :] = back
        source = back * gain_t[here, :]
        src1_t[here, :] = source
        return xa, decay1 * xb + source[None]

    unused, s1 = lax.fori_loop(0, LOCAL, middle, (c2, zero), unroll=UNROLL)
    keep[S1] = s1
    vsend[0, 0] = s1
    send(0, vsend, vrecv, vs_sem, vr_sem)

    unused, m1, l01, l11 = near(src1_t, sig1_t, decay1)
    wait_bytes(yrecv.at[pl.ds(0, 3)], n_sem.at[3])
    y1, y11, y2 = (yrecv[:, k].reshape(STATE) for k in range(3))
    rate1, amp1 = keep[RATE1], keep[AMP1]
    zero_sum = l01 + s1 * y1
    one_sum = l11 + s1 * y11 + m1 * y1
    grads[0] = zero_sum * jnp.sqrt(2.0 * rate1) * SCALE
    grads[1] = amp1 * (0.5 * zero_sum - rate1 * one_sum) * SCALE
    rate2, amp2 = keep[RATE2], keep[AMP2]
    c2 = keep[C2]
    zero_sum = keep[L02] + keep[ZA2] * c2
    one_sum = keep[L12] + keep[ZB2] * c2 + keep[M2] * y2 + (128.0 * jnp.exp(-128.0 * rate2)) * (y2 * c2)
    grads[2] = zero_sum * jnp.sqrt(2.0 * rate2) * SCALE
    grads[3] = amp2 * (0.5 * zero_sum - rate2 * one_sum) * SCALE

    def share(ref, q):
        return ref.at[q // 4, pl.ds((q % 4) * 2, 2)]

    for i, q in enumerate(plane):
        pltpu.make_async_remote_copy(
            src_ref=share(grads, q), dst_ref=rs_recv.at[i], send_sem=p_send.at[0], recv_sem=p_recv.at[0],
            device_id=(dp, q * 4 + z), device_id_type=MESH,
        ).start()

    back_step(0, vsend, vrecv, vs_sem, vr_sem, S1, RATE1)

    wait_bytes(rs_recv, p_recv.at[0])
    total = grads[me // 4, pl.ds((me % 4) * 2, 2)]
    for i in range(15):
        total = total + rs_recv[i]
    zred[z] = total
    for d in (1, 2, 3):
        pltpu.make_async_remote_copy(
            src_ref=zred.at[z], dst_ref=zred.at[z], send_sem=p_send.at[1], recv_sem=p_recv.at[1],
            device_id=at(2, d), device_id_type=MESH,
        ).start()

    back_step(1, vsend, vrecv, vs_sem, vr_sem, S1, RATE1)

    outs = (value_out, key1_out, gate1_out, key2_out, gate2_out)

    def emit(i):
        pltpu.make_async_copy(made.at[i], outs[i].at[0], out_sem.at[i]).start()

    def store(i, c, tile):
        made[i, c * 128 : (c + 1) * 128, :] = tile.astype(jnp.bfloat16)

    for c in range(4):
        back = back2_t[pl.ds(c, LOCAL, stride=8), :].T
        store(2, c, back * block(2, c) * block(4, c))
        store(3, c, back * (block(3, c) * block(4, c)))
        store(4, c, block(0, c) * block(7, c))
    for i in (2, 3, 4):
        emit(i)

    wait_bytes(zred.at[pl.ds(0, 3)], p_recv.at[1])
    total = (zred[0] + zred[1]) + (zred[2] + zred[3])
    piece[...] = total
    sums[me] = total
    for i, q in enumerate(plane):
        pltpu.make_async_remote_copy(
            src_ref=piece, dst_ref=sums.at[me], send_sem=p_send.at[2], recv_sem=p_recv.at[2],
            device_id=(dp, q * 4 + z), device_id_type=MESH,
        ).start()

    c1 = back_step(2, vsend, vrecv, vs_sem, vr_sem, S1, RATE1)
    decay1 = jnp.exp(-keep[RATE1])
    amp1 = keep[AMP1]

    def last(i, xa):
        t = LOCAL - 1 - i
        xa = decay1 * xa + row(src1_t, t)
        part = jnp.sum(amp1 * xa, axis=0)
        back1_t[pl.ds(pl.multiple_of(t * 8, 8), 8), :] = part + pltpu.roll(part, 4, 0)
        return xa

    lax.fori_loop(0, LOCAL, last, c1, unroll=UNROLL)
    for c in range(4):
        back = back1_t[pl.ds(c, LOCAL, stride=8), :].T
        store(0, c, back * block(5, c))
        store(1, c, back * block(6, c))
    for i in (0, 1):
        emit(i)

    wait_bytes(sums.at[pl.ds(0, 15)], p_recv.at[2])
    last_copy = pltpu.make_async_copy(sums, sums_out, out_sem.at[5])
    last_copy.start()
    for axis in range(3):
        wait_bytes(urecv.at[axis], us_sem.at[axis])
        wait_bytes(vrecv.at[axis], vs_sem.at[axis])
    wait_bytes(nrecv.at[pl.ds(0, 3)], n_sem.at[0])
    wait_bytes(yrecv.at[pl.ds(0, 3)], n_sem.at[2])
    for k in range(1, 16):
        @pl.when(me + k < 16)
        def _():
            wait_bytes(tsend, ts_sem.at[k - 1])
    wait_bytes(rs_recv, p_send.at[0])
    wait_bytes(zred.at[pl.ds(0, 3)], p_send.at[1])
    wait_bytes(rs_recv, p_send.at[2])
    for i in range(5):
        pltpu.make_async_copy(made.at[i], outs[i].at[0], out_sem.at[i]).wait()
    last_copy.wait()


def hand_over(*refs):
    made, sums, outs, held, turned, thin, sem_in, sem_out = refs[:5], refs[5], refs[6:15], *refs[15:]
    loads = [pltpu.make_async_copy(made[i], held.at[i], sem_in.at[i]) for i in range(5)]
    loads.append(pltpu.make_async_copy(sums, turned, sem_in.at[5]))
    stores = [pltpu.make_async_copy(held.at[i], outs[i], sem_out.at[i]) for i in range(5)]
    stores += [pltpu.make_async_copy(thin.at[i], outs[5 + i], sem_out.at[5 + i]) for i in range(4)]
    for load in loads:
        load.start()
    for i in range(5):
        loads[i].wait()
        stores[i].start()
    loads[5].wait()
    for i in range(4):
        for c in range(4):
            thin[i, :, c * 128 : (c + 1) * 128] = turned[pl.ds(i * 64 + c, ORDER, stride=4), :]
        stores[5 + i].start()
    for store in stores:
        store.wait()


def per_device(
    value, key_one, gate_one, conv_one, key_two, gate_two, conv_two, grad_out,
    residues_one, log_rate_one, residues_two, log_rate_two,
):
    f32 = jnp.float32
    vmem = pltpu.VMEM
    dma = pltpu.SemaphoreType.DMA
    turned = vmem((LOCAL * 8, 128), f32)
    bf16 = jnp.bfloat16
    shape = value.shape
    anywhere = pl.BlockSpec(memory_space=pl.ANY)
    made = pl.pallas_call(
        kernel,
        out_shape=[jax.ShapeDtypeStruct(shape, bf16)] * 5 + [jax.ShapeDtypeStruct((16, 2, 8, 128), f32)],
        in_specs=[anywhere] * 12,
        out_specs=[anywhere] * 6,
        scratch_shapes=[
            vmem((8, CHAN, LOCAL), bf16),
            vmem((4, ORDER, CHAN), f32),
            vmem((5, CHAN, LOCAL), bf16),
            vmem((16, 2, 8, 128), f32),
            dma((12,)),
            turned, turned, turned, turned, turned, turned, turned,
            vmem((4, 64, 128), f32),
            vmem((13,) + STATE, f32),
            vmem((3, 2) + STATE, f32),
            vmem((3, 3) + STATE, f32),
            vmem((4, 3, 2, 8, 128), f32),
            vmem((4, 3, 2, 8, 128), f32),
            vmem((3, 2, 8, 128), f32),
            vmem((15, 3, 2, 8, 128), f32),
            vmem((4, 3, 2, 8, 128), f32),
            vmem((4, 3, 2, 8, 128), f32),
            vmem((3, 2) + STATE, f32),
            vmem((3, 3) + STATE, f32),
            vmem((4,) + STATE, f32),
            vmem((15, 2, 8, 128), f32),
            vmem((4, 2, 8, 128), f32),
            vmem((2, 8, 128), f32),
            dma((3,)), dma((3,)), dma((4,)), dma((15,)), dma((15,)), dma((3,)), dma((3,)), dma((3,)), dma((3,)), dma((6,)),
        ],
        compiler_params=pltpu.CompilerParams(
            collective_id=0, has_side_effects=True, vmem_limit_bytes=56 * 1024 * 1024
        ),
        name="hyena_back",
    )(
        value, key_one, gate_one, conv_one, key_two, gate_two, conv_two, grad_out,
        residues_one.T, log_rate_one.T, residues_two.T, log_rate_two.T,
    )
    made = list(made[:5]) + [made[5].reshape(4 * ORDER * 4, 128)]
    thin = jax.ShapeDtypeStruct((ORDER, CHAN), f32)
    outs = pl.pallas_call(
        hand_over,
        out_shape=[jax.ShapeDtypeStruct(shape, bf16)] * 5 + [thin] * 4,
        in_specs=[anywhere] * 6,
        out_specs=[anywhere] * 9,
        scratch_shapes=[
            vmem((5,) + shape, bf16),
            vmem((4 * ORDER * 4, 128), f32),
            vmem((4, ORDER, CHAN), f32),
            dma((6,)),
            dma((9,)),
        ],
        name="hand_over",
    )(*made)
    return tuple(outs[:5]) + tuple(out.T for out in outs[5:])


def solution(mesh):
    wide = P(None, "dp", "context")
    thin = P("dp", None)
    return jax.shard_map(
        per_device,
        mesh=mesh,
        in_specs=(wide,) * 8 + (thin,) * 4,
        out_specs=(wide,) * 5 + (thin,) * 4,
        check_vma=False,
    )
```

time: 78.8 us -> 62.3 us (0.79); the launches traced: 77.7 us -> 62.1 us
  Pallas kernels: 70.7 us -> 61.5 us
  local copies, waits for them, and re-layouts: 4.66 us -> 0 us
  other arithmetic: 1.57 us -> 0 us
    pallas_call x1 -> x2, Pallas kernels: 70.7 us -> 61.5 us  [the longest x1 59.5 us: per_device(): pl.pallas_call(kernel, out_shape=[jax.ShapeDtypeStruct(shape, bf16)] * 5...]
    unnamed x26 -> x0, local copies, waits for them, and re-layouts: 3.39 us -> none
    convert_element_type x2 -> x0, other arithmetic: 1.57 us -> none  [rounded(): return array.astype(jnp.bfloat16)]
    squeeze x2 -> x0, local copies, waits for them, and re-layouts: 1.26 us -> none  [the longest x1 0.63 us: per_device(): grads[3]]
where the time goes in v2:
time: 62.3 us; the launch traced here: 62.1 us
  Pallas kernels  61.5 us (99%)
  between operations  0.65 us (1%)
    pallas_call x1, Pallas kernels, per_device(): pl.pallas_call(kernel, out_shape=[jax.ShapeDtypeStruct(shape, bf16)] * 5...  59.5 us
    pallas_call x1, Pallas kernels, per_device(): pl.pallas_call(hand_over, out_shape=[jax.ShapeDtypeStruct(shape, bf16)] *...  1.99 us

profile of v2, /device:TPU:6, one launch (start us, length us, event | category | flops | bytes accessed | tf_op | source)
XLA Modules:
  0.0 62.1 jit_solution(1542105497905147096)
XLA Ops:
  0.6 59.5 %hyena_back.1 = (bf16[1,512,128]{2,1,0:T(8,128)(2,1)}, bf16[1,512,128]{2,1,0:T(8,128)(2,1)}, bf16[1,512,128]{2,1,0:T(8,128)(2,1)}, bf16[1,512,128]{2,1,0:T(8,128...) custom-call(bf16[1,512,128]{2,1,0:T(8,128)(2,1)} %value.1, bf16[1,512,128]{2,1,0:T(8,128)(2,1)} %key_one.1, ...), custom_call_target="tpu_custom_call" | custom-call | tf_op jit(solution)/shard_map/hyena_back/pallas_call | solution.py:404
  60.1 2.0 %hand_over.1 = (bf16[1,512,128]{2,1,0:T(8,128)(2,1)}, bf16[1,512,128]{2,1,0:T(8,128)(2,1)}, bf16[1,512,128]{2,1,0:T(8,128)(2,1)}, bf16[1,512,128]{2,1,0:T(8,128)...) custom-call(bf16[1,512,128]{2,1,0:T(8,128)(2,1)} %get-tuple-element., ...), custom_call_target="tpu_custom_call" | custom-call | tf_op jit(solution)/shard_map/hand_over/pallas_call | solution.py:444

commit v3 on v2

--- a/solution.py
+++ b/solution.py
@@ -13,9 +13,10 @@
 ORDER = 16
 STATE = (8, 8, 128)
 SCALE = 1.0 / math.sqrt(8192.0)
-UNROLL = 4
-
-(AMP1, RATE1, AMP2, RATE2, S2, M2, L02, L12, ZA2, ZB2, C2, S1, EU) = range(13)
+UNROLL = 8
+CUTS = 2
+
+(AMP1, RATE1, AMP2, RATE2, S2, M2, L02, L12, ZA2, ZB2, C2, S1, EU, POW1, POW2) = (*range(13), 13, 16)
 
 
 def wait_bytes(ref, sem):
@@ -25,7 +26,7 @@
 def kernel(
     value, key_one, gate_one, conv_one, key_two, gate_two, conv_two, grad_out, res1, lr1, res2, lr2,
     value_out, key1_out, gate1_out, key2_out, gate2_out, sums_out,
-    wide, narrow, made, sums, in_sem, src2_t, gain_t, sig1_t, sig2_t, src1_t, back2_t, back1_t, par,
+    wide, narrow, made, in_sem, src2_t, gain_t, sig1_t, sig2_t, src1_t, back2_t, back1_t, par,
     keep, usend, urecv, nsend, nrecv, tsend, trecv, ysend, yrecv, vsend, vrecv, grads, rs_recv, zred, piece,
     us_sem, ur_sem, n_sem, ts_sem, tr_sem, vs_sem, vr_sem, p_send, p_recv, out_sem,
 ):
@@ -43,14 +44,20 @@
         return (dp, y * 16 + x * 4 + (z + d) % 4)
 
     plane = [
-        (((y + e) % 4) * 4 + (x + f) % 4) for e in range(4) for f in range(4) if e or f
+        (((y + e) % 4) * 4 + (x + f) % 4) for e in (2, 1, 3, 0) for f in (2, 1, 3, 0) if e or f
     ]
 
     barrier = pltpu.get_barrier_semaphore()
-    for q in plane:
-        pl.semaphore_signal(barrier, inc=1, device_id=(dp, q * 4 + z), device_id_type=MESH)
-    for d in (1, 2, 3):
+    for d in (2, 1, 3):
         pl.semaphore_signal(barrier, inc=1, device_id=at(2, d), device_id_type=MESH)
+
+    trecv[...] = jnp.zeros(trecv.shape, jnp.float32)
+    urecv[0] = jnp.zeros(urecv.shape[1:], jnp.float32)
+    vrecv[0] = jnp.zeros(vrecv.shape[1:], jnp.float32)
+
+    for axis in (0, 1):
+        for d in (2, 1, 3):
+            pl.semaphore_signal(barrier, inc=1, device_id=at(axis, d), device_id_type=MESH)
 
     wide_in = (grad_out, gate_two, key_two, gate_one, conv_one, key_one, value, conv_two)
     narrow_in = (lr2, lr1, res2, res1)
@@ -121,34 +128,52 @@
     for k, array in enumerate((za1, zb1, za2)):
         nsend[:, k] = array.reshape(4, 2, 8, 128)
 
-    pl.semaphore_wait(barrier, 18)
+    pl.semaphore_wait(barrier, 9)
 
     def send(axis, buf, recv, ssem, rsem):
-        for d in (1, 2, 3):
-            which = 0 if axis == 0 else (coords[axis] + d) // 4
-            pltpu.make_async_remote_copy(
-                src_ref=buf.at[axis, which],
+        for d in (2, 1, 3):
+            copy = pltpu.make_async_remote_copy(
+                src_ref=buf.at[axis, 0 if axis == 0 else (coords[axis] + d) // 4],
                 dst_ref=recv.at[axis, 3 - d],
-                send_sem=ssem.at[axis],
-                recv_sem=rsem.at[axis],
+                send_sem=ssem.at[d - 1 if axis == 0 else axis + 2],
+                recv_sem=rsem.at[3 - d if axis == 0 else axis + 2],
                 device_id=at(axis, d),
                 device_id_type=MESH,
-            ).start()
+            )
+            if axis:
+                copy.start()
+            else:
+                pl.when(y + d >= 4)(copy.start)
+
+    def arrived(axis, recv, rsem):
+        if axis:
+            wait_bytes(recv.at[axis], rsem.at[axis + 2])
+        else:
+            for d in (1, 2, 3):
+                @pl.when(y + d < 4)
+                def _():
+                    wait_bytes(recv.at[0, d - 1], rsem.at[d - 1])
+
+    def departed(axis, recv, ssem):
+        if axis:
+            wait_bytes(recv.at[axis], ssem.at[axis + 2])
+        else:
+            for d in (1, 2, 3):
+                @pl.when(y + d >= 4)
+                def _():
+                    wait_bytes(recv.at[0, d - 1], ssem.at[d - 1])
 
     strides = (2048.0, 512.0, 128.0)
 
-    def masked(axis, array, d):
-        return array if axis else jnp.where(y + d < 4, array, 0.0)
-
     def suffix_merge(axis, recv, rsem, far, rate):
-        wait_bytes(recv.at[axis], rsem.at[axis])
-        power = jnp.exp(-strides[axis] * rate)
+        arrived(axis, recv, rsem)
+        power = keep[rate + axis]
         for d in (3, 2, 1):
-            far = masked(axis, recv[axis, d - 1], d) + power * far
+            far = recv[axis, d - 1] + power * far
         return far, power
 
     def spread_signals():
-        for d in (1, 2, 3):
+        for d in (2, 1, 3):
             pltpu.make_async_remote_copy(
                 src_ref=nsend.at[(z + d) % 4], dst_ref=nrecv.at[z], send_sem=n_sem.at[0], recv_sem=n_sem.at[1],
                 device_id=at(2, d), device_id_type=MESH,
@@ -176,7 +201,7 @@
             state = added(line(i), shifted(state, 128.0, powers))
         for k in range(3):
             tsend[k] = state[k]
-        for k in range(1, 16):
+        for k in range(15, 0, -1):
             @pl.when(me + k < 16)
             def _():
                 pltpu.make_async_remote_copy(
@@ -197,14 +222,13 @@
                 wait_bytes(trecv.at[k - 1], tr_sem.at[k - 1])
         state = tuple(jnp.zeros((2, 8, 128), jnp.float32) for _ in range(3))
         for k in range(15, 0, -1):
-            there = me >= k
-            block = tuple(jnp.where(there, trecv[k - 1, i], 0.0) for i in range(3))
+            block = tuple(trecv[k - 1, i] for i in range(3))
             state = added(block, shifted(state, 512.0, powers))
         for i in range(4):
             for k in range(3):
                 ysend[i, k] = state[k]
             state = added(line(i), shifted(state, 128.0, near_powers))
-        for d in (1, 2, 3):
+        for d in (2, 1, 3):
             pltpu.make_async_remote_copy(
                 src_ref=ysend.at[(z + d) % 4], dst_ref=yrecv.at[z], send_sem=n_sem.at[2], recv_sem=n_sem.at[3],
                 device_id=at(2, d), device_id_type=MESH,
@@ -213,7 +237,7 @@
 
     def back_step(axis, buf, recv, ssem, rsem, own, rate):
         far = zero if axis == 0 else keep[EU]
-        far, power = suffix_merge(axis, recv, rsem, far, keep[rate])
+        far, power = suffix_merge(axis, recv, rsem, far, rate)
         keep[EU] = far
         if axis < 2:
             buf[axis + 1, 0] = far
@@ -223,6 +247,10 @@
 
     send(0, usend, urecv, us_sem, ur_sem)
     spread_signals()
+
+    for axis, step in enumerate(strides):
+        keep[POW2 + axis] = jnp.exp(-step * rate2)
+        keep[POW1 + axis] = jnp.exp(-step * keep[RATE1])
 
     def near(src_t, sig_t, decay):
         def body(i, st):
@@ -238,11 +266,11 @@
     unused, m2, l02, l12 = near(src2_t, sig2_t, decay2)
     keep[M2], keep[L02], keep[L12] = m2, l02, l12
 
-    back_step(0, usend, urecv, us_sem, ur_sem, S2, RATE2)
-    back_step(1, usend, urecv, us_sem, ur_sem, S2, RATE2)
+    back_step(0, usend, urecv, us_sem, ur_sem, S2, POW2)
+    back_step(1, usend, urecv, us_sem, ur_sem, S2, POW2)
     total_lines()
     return_signals()
-    c2 = back_step(2, usend, urecv, us_sem, ur_sem, S2, RATE2)
+    c2 = back_step(2, usend, urecv, us_sem, ur_sem, S2, POW2)
     keep[C2] = c2
 
     decay1 = jnp.exp(-keep[RATE1])
@@ -267,19 +295,26 @@
     send(0, vsend, vrecv, vs_sem, vr_sem)
 
     unused, m1, l01, l11 = near(src1_t, sig1_t, decay1)
+    back_step(0, vsend, vrecv, vs_sem, vr_sem, S1, POW1)
+    rate1, amp1 = keep[RATE1], keep[AMP1]
+    rate2, amp2 = keep[RATE2], keep[AMP2]
+    c2 = keep[C2]
+    root1 = jnp.sqrt(2.0 * rate1) * SCALE
+    half1, turn1 = amp1 * (0.5 * SCALE), amp1 * rate1 * SCALE
+    zero_sum = keep[L02] + keep[ZA2] * c2
+    one_sum = keep[L12] + keep[ZB2] * c2
+    far2 = keep[M2] + (128.0 * keep[POW2 + 2]) * c2
+    turn2 = amp2 * rate2 * SCALE
+    grads[2] = zero_sum * jnp.sqrt(2.0 * rate2) * SCALE
+    grads[3] = amp2 * (0.5 * SCALE) * zero_sum - turn2 * one_sum
+    far2 = turn2 * far2
     wait_bytes(yrecv.at[pl.ds(0, 3)], n_sem.at[3])
     y1, y11, y2 = (yrecv[:, k].reshape(STATE) for k in range(3))
-    rate1, amp1 = keep[RATE1], keep[AMP1]
     zero_sum = l01 + s1 * y1
     one_sum = l11 + s1 * y11 + m1 * y1
-    grads[0] = zero_sum * jnp.sqrt(2.0 * rate1) * SCALE
-    grads[1] = amp1 * (0.5 * zero_sum - rate1 * one_sum) * SCALE
-    rate2, amp2 = keep[RATE2], keep[AMP2]
-    c2 = keep[C2]
-    zero_sum = keep[L02] + keep[ZA2] * c2
-    one_sum = keep[L12] + keep[ZB2] * c2 + keep[M2] * y2 + (128.0 * jnp.exp(-128.0 * rate2)) * (y2 * c2)
-    grads[2] = zero_sum * jnp.sqrt(2.0 * rate2) * SCALE
-    grads[3] = amp2 * (0.5 * zero_sum - rate2 * one_sum) * SCALE
+    grads[0] = zero_sum * root1
+    grads[1] = half1 * zero_sum - turn1 * one_sum
+    grads[3] = grads[3] - far2 * y2
 
     def share(ref, q):
         return ref.at[q // 4, pl.ds((q % 4) * 2, 2)]
@@ -290,21 +325,8 @@
             device_id=(dp, q * 4 + z), device_id_type=MESH,
         ).start()
 
-    back_step(0, vsend, vrecv, vs_sem, vr_sem, S1, RATE1)
-
-    wait_bytes(rs_recv, p_recv.at[0])
-    total = grads[me // 4, pl.ds((me % 4) * 2, 2)]
-    for i in range(15):
-        total = total + rs_recv[i]
-    zred[z] = total
-    for d in (1, 2, 3):
-        pltpu.make_async_remote_copy(
-            src_ref=zred.at[z], dst_ref=zred.at[z], send_sem=p_send.at[1], recv_sem=p_recv.at[1],
-            device_id=at(2, d), device_id_type=MESH,
-        ).start()
-
-    back_step(1, vsend, vrecv, vs_sem, vr_sem, S1, RATE1)
-
+
+    back_step(1, vsend, vrecv, vs_sem, vr_sem, S1, POW1)
     outs = (value_out, key1_out, gate1_out, key2_out, gate2_out)
 
     def emit(i):
@@ -321,17 +343,19 @@
     for i in (2, 3, 4):
         emit(i)
 
-    wait_bytes(zred.at[pl.ds(0, 3)], p_recv.at[1])
-    total = (zred[0] + zred[1]) + (zred[2] + zred[3])
-    piece[...] = total
-    sums[me] = total
-    for i, q in enumerate(plane):
+    wait_bytes(rs_recv, p_recv.at[0])
+    total = grads[me // 4, pl.ds((me % 4) * 2, 2)]
+    for i in range(15):
+        total = total + rs_recv[i]
+    zred[z] = total
+    for d in (2, 1, 3):
         pltpu.make_async_remote_copy(
-            src_ref=piece, dst_ref=sums.at[me], send_sem=p_send.at[2], recv_sem=p_recv.at[2],
-            device_id=(dp, q * 4 + z), device_id_type=MESH,
+            src_ref=zred.at[z], dst_ref=zred.at[z], send_sem=p_send.at[1], recv_sem=p_recv.at[1],
+            device_id=at(2, d), device_id_type=MESH,
         ).start()
 
-    c1 = back_step(2, vsend, vrecv, vs_sem, vr_sem, S1, RATE1)
+
+    c1 = back_step(2, vsend, vrecv, vs_sem, vr_sem, S1, POW1)
     decay1 = jnp.exp(-keep[RATE1])
     amp1 = keep[AMP1]
 
@@ -343,6 +367,17 @@
         return xa
 
     lax.fori_loop(0, LOCAL, last, c1, unroll=UNROLL)
+    wait_bytes(zred.at[pl.ds(0, 3)], p_recv.at[1])
+    total = (zred[0] + zred[1]) + (zred[2] + zred[3])
+    piece[...] = total
+    own = pltpu.make_async_copy(piece, sums_out.at[me], out_sem.at[5])
+    own.start()
+    for i, q in enumerate(plane):
+        pltpu.make_async_remote_copy(
+            src_ref=piece, dst_ref=sums_out.at[me], send_sem=p_send.at[2], recv_sem=p_recv.at[2],
+            device_id=(dp, q * 4 + z), device_id_type=MESH,
+        ).start()
+
     for c in range(4):
         back = back1_t[pl.ds(c, LOCAL, stride=8), :].T
         store(0, c, back * block(5, c))
@@ -350,12 +385,10 @@
     for i in (0, 1):
         emit(i)
 
-    wait_bytes(sums.at[pl.ds(0, 15)], p_recv.at[2])
-    last_copy = pltpu.make_async_copy(sums, sums_out, out_sem.at[5])
-    last_copy.start()
+    wait_bytes(sums_out.at[pl.ds(0, 15)], p_recv.at[2])
     for axis in range(3):
-        wait_bytes(urecv.at[axis], us_sem.at[axis])
-        wait_bytes(vrecv.at[axis], vs_sem.at[axis])
+        departed(axis, urecv, us_sem)
+        departed(axis, vrecv, vs_sem)
     wait_bytes(nrecv.at[pl.ds(0, 3)], n_sem.at[0])
     wait_bytes(yrecv.at[pl.ds(0, 3)], n_sem.at[2])
     for k in range(1, 16):
@@ -367,25 +400,32 @@
     wait_bytes(rs_recv, p_send.at[2])
     for i in range(5):
         pltpu.make_async_copy(made.at[i], outs[i].at[0], out_sem.at[i]).wait()
-    last_copy.wait()
+    own.wait()
 
 
 def hand_over(*refs):
     made, sums, outs, held, turned, thin, sem_in, sem_out = refs[:5], refs[5], refs[6:15], *refs[15:]
-    loads = [pltpu.make_async_copy(made[i], held.at[i], sem_in.at[i]) for i in range(5)]
-    loads.append(pltpu.make_async_copy(sums, turned, sem_in.at[5]))
-    stores = [pltpu.make_async_copy(held.at[i], outs[i], sem_out.at[i]) for i in range(5)]
-    stores += [pltpu.make_async_copy(thin.at[i], outs[5 + i], sem_out.at[5 + i]) for i in range(4)]
+    rows = CHAN // CUTS
+    loads, stores = [], []
+    for i in range(5):
+        for j in range(CUTS):
+            here = (i, 0, pl.ds(j * rows, rows))
+            there = (0, pl.ds(j * rows, rows))
+            loads.append(pltpu.make_async_copy(made[i].at[there], held.at[here], sem_in.at[len(loads)]))
+            stores.append(pltpu.make_async_copy(held.at[here], outs[i].at[there], sem_out.at[len(stores)]))
+    last = pltpu.make_async_copy(sums, turned, sem_in.at[len(loads)])
+    last.start()
     for load in loads:
         load.start()
-    for i in range(5):
-        loads[i].wait()
-        stores[i].start()
-    loads[5].wait()
+    last.wait()
     for i in range(4):
         for c in range(4):
             thin[i, :, c * 128 : (c + 1) * 128] = turned[pl.ds(i * 64 + c, ORDER, stride=4), :]
-        stores[5 + i].start()
+        stores.append(pltpu.make_async_copy(thin.at[i], outs[5 + i], sem_out.at[len(stores)]))
+        stores[-1].start()
+    for load, store in zip(loads, stores):
+        load.wait()
+        store.start()
     for store in stores:
         store.wait()
 
@@ -410,11 +450,10 @@
             vmem((8, CHAN, LOCAL), bf16),
             vmem((4, ORDER, CHAN), f32),
             vmem((5, CHAN, LOCAL), bf16),
-            vmem((16, 2, 8, 128), f32),
             dma((12,)),
             turned, turned, turned, turned, turned, turned, turned,
             vmem((4, 64, 128), f32),
-            vmem((13,) + STATE, f32),
+            vmem((19,) + STATE, f32),
             vmem((3, 2) + STATE, f32),
             vmem((3, 3) + STATE, f32),
             vmem((4, 3, 2, 8, 128), f32),
@@ -429,7 +468,7 @@
             vmem((15, 2, 8, 128), f32),
             vmem((4, 2, 8, 128), f32),
             vmem((2, 8, 128), f32),
-            dma((3,)), dma((3,)), dma((4,)), dma((15,)), dma((15,)), dma((3,)), dma((3,)), dma((3,)), dma((3,)), dma((6,)),
+            dma((5,)), dma((5,)), dma((4,)), dma((15,)), dma((15,)), dma((5,)), dma((5,)), dma((3,)), dma((3,)), dma((6,)),
         ],
         compiler_params=pltpu.CompilerParams(
             collective_id=0, has_side_effects=True, vmem_limit_bytes=56 * 1024 * 1024
@@ -450,8 +489,8 @@
             vmem((5,) + shape, bf16),
             vmem((4 * ORDER * 4, 128), f32),
             vmem((4, ORDER, CHAN), f32),
-            dma((6,)),
-            dma((9,)),
+            dma((5 * CUTS + 1,)),
+            dma((5 * CUTS + 4,)),
         ],
         name="hand_over",
     )(*made)

time: 62.3 us -> 58.1 us (0.933)
  Pallas kernels: 61.5 us -> 56.7 us
    pallas_call x1, Pallas kernels: 59.5 us -> 54.7 us  [per_device(): pl.pallas_call(kernel, out_shape=[jax.ShapeDtypeStruct(shape, bf16)] * 5...]
where the time goes in v3:
time: 58.1 us; the launch traced here: 57.3 us
  Pallas kernels  56.7 us (98%)
  between operations  0.65 us (1%)
    pallas_call x1, Pallas kernels, per_device(): pl.pallas_call(kernel, out_shape=[jax.ShapeDtypeStruct(shape, bf16)] * 5...  54.7 us
    pallas_call x1, Pallas kernels, per_device(): pl.pallas_call(hand_over, out_shape=[jax.ShapeDtypeStruct(shape, bf16)] *...  2.01 us

profile of v3, /device:TPU:6, one launch (start us, length us, event | category | flops | bytes accessed | tf_op | source)
XLA Modules:
  0.0 57.3 jit_solution(5124455793895946858)
XLA Ops:
  0.6 54.7 %hyena_back.1 = (bf16[1,512,128]{2,1,0:T(8,128)(2,1)}, bf16[1,512,128]{2,1,0:T(8,128)(2,1)}, bf16[1,512,128]{2,1,0:T(8,128)(2,1)}, bf16[1,512,128]{2,1,0:T(8,128...) custom-call(bf16[1,512,128]{2,1,0:T(8,128)(2,1)} %value.1, bf16[1,512,128]{2,1,0:T(8,128)(2,1)} %key_one.1, ...), custom_call_target="tpu_custom_call" | custom-call | tf_op jit(solution)/shard_map/hyena_back/pallas_call | solution.py:444
  55.3 2.0 %hand_over.1 = (bf16[1,512,128]{2,1,0:T(8,128)(2,1)}, bf16[1,512,128]{2,1,0:T(8,128)(2,1)}, bf16[1,512,128]{2,1,0:T(8,128)(2,1)}, bf16[1,512,128]{2,1,0:T(8,128)...) custom-call(bf16[1,512,128]{2,1,0:T(8,128)(2,1)} %get-tuple-element., ...), custom_call_target="tpu_custom_call" | custom-call | tf_op jit(solution)/shard_map/hand_over/pallas_call | solution.py:483

commit v4 on v3

--- a/solution.py
+++ b/solution.py
@@ -14,7 +14,6 @@
 STATE = (8, 8, 128)
 SCALE = 1.0 / math.sqrt(8192.0)
 UNROLL = 8
-CUTS = 2
 
 (AMP1, RATE1, AMP2, RATE2, S2, M2, L02, L12, ZA2, ZB2, C2, S1, EU, POW1, POW2) = (*range(13), 13, 16)
 
@@ -26,9 +25,9 @@
 def kernel(
     value, key_one, gate_one, conv_one, key_two, gate_two, conv_two, grad_out, res1, lr1, res2, lr2,
     value_out, key1_out, gate1_out, key2_out, gate2_out, sums_out,
-    wide, narrow, made, in_sem, src2_t, gain_t, sig1_t, sig2_t, src1_t, back2_t, back1_t, par,
+    wide, narrow, in_sem, src2_t, gain_t, sig1_t, sig2_t, src1_t, back2_t, back1_t, par,
     keep, usend, urecv, nsend, nrecv, tsend, trecv, ysend, yrecv, vsend, vrecv, grads, rs_recv, zred, piece,
-    us_sem, ur_sem, n_sem, ts_sem, tr_sem, vs_sem, vr_sem, p_send, p_recv, out_sem,
+    us_sem, ur_sem, n_sem, ts_sem, tr_sem, vs_sem, vr_sem, p_send, p_recv,
 ):
     dp = lax.axis_index("dp")
     ctx = lax.axis_index("context")
@@ -245,8 +244,8 @@
             send(axis + 1, buf, recv, ssem, rsem)
         return far
 
+    spread_signals()
     send(0, usend, urecv, us_sem, ur_sem)
-    spread_signals()
 
     for axis, step in enumerate(strides):
         keep[POW2 + axis] = jnp.exp(-step * rate2)
@@ -327,22 +326,6 @@
 
 
     back_step(1, vsend, vrecv, vs_sem, vr_sem, S1, POW1)
-    outs = (value_out, key1_out, gate1_out, key2_out, gate2_out)
-
-    def emit(i):
-        pltpu.make_async_copy(made.at[i], outs[i].at[0], out_sem.at[i]).start()
-
-    def store(i, c, tile):
-        made[i, c * 128 : (c + 1) * 128, :] = tile.astype(jnp.bfloat16)
-
-    for c in range(4):
-        back = back2_t[pl.ds(c, LOCAL, stride=8), :].T
-        store(2, c, back * block(2, c) * block(4, c))
-        store(3, c, back * (block(3, c) * block(4, c)))
-        store(4, c, block(0, c) * block(7, c))
-    for i in (2, 3, 4):
-        emit(i)
-
     wait_bytes(rs_recv, p_recv.at[0])
     total = grads[me // 4, pl.ds((me % 4) * 2, 2)]
     for i in range(15):
@@ -354,6 +337,27 @@
             device_id=at(2, d), device_id_type=MESH,
         ).start()
 
+    outs = (value_out, key1_out, gate1_out, key2_out, gate2_out)
+
+    def store(i, c, tile):
+        outs[i][0, c * 128 : (c + 1) * 128, :] = tile.astype(jnp.bfloat16)
+
+    for c in range(4):
+        back = back2_t[pl.ds(c, LOCAL, stride=8), :].T
+        store(2, c, back * block(2, c) * block(4, c))
+        store(3, c, back * (block(3, c) * block(4, c)))
+        store(4, c, block(0, c) * block(7, c))
+
+
+    wait_bytes(zred.at[pl.ds(0, 3)], p_recv.at[1])
+    total = (zred[0] + zred[1]) + (zred[2] + zred[3])
+    piece[...] = total
+    sums_out[me] = total
+    for i, q in enumerate(plane):
+        pltpu.make_async_remote_copy(
+            src_ref=piece, dst_ref=sums_out.at[me], send_sem=p_send.at[2], recv_sem=p_recv.at[2],
+            device_id=(dp, q * 4 + z), device_id_type=MESH,
+        ).start()
 
     c1 = back_step(2, vsend, vrecv, vs_sem, vr_sem, S1, POW1)
     decay1 = jnp.exp(-keep[RATE1])
@@ -367,23 +371,10 @@
         return xa
 
     lax.fori_loop(0, LOCAL, last, c1, unroll=UNROLL)
-    wait_bytes(zred.at[pl.ds(0, 3)], p_recv.at[1])
-    total = (zred[0] + zred[1]) + (zred[2] + zred[3])
-    piece[...] = total
-    own = pltpu.make_async_copy(piece, sums_out.at[me], out_sem.at[5])
-    own.start()
-    for i, q in enumerate(plane):
-        pltpu.make_async_remote_copy(
-            src_ref=piece, dst_ref=sums_out.at[me], send_sem=p_send.at[2], recv_sem=p_recv.at[2],
-            device_id=(dp, q * 4 + z), device_id_type=MESH,
-        ).start()
-
     for c in range(4):
         back = back1_t[pl.ds(c, LOCAL, stride=8), :].T
         store(0, c, back * block(5, c))
         store(1, c, back * block(6, c))
-    for i in (0, 1):
-        emit(i)
 
     wait_bytes(sums_out.at[pl.ds(0, 15)], p_recv.at[2])
     for axis in range(3):
@@ -398,34 +389,18 @@
     wait_bytes(rs_recv, p_send.at[0])
     wait_bytes(zred.at[pl.ds(0, 3)], p_send.at[1])
     wait_bytes(rs_recv, p_send.at[2])
-    for i in range(5):
-        pltpu.make_async_copy(made.at[i], outs[i].at[0], out_sem.at[i]).wait()
-    own.wait()
 
 
 def hand_over(*refs):
-    made, sums, outs, held, turned, thin, sem_in, sem_out = refs[:5], refs[5], refs[6:15], *refs[15:]
-    rows = CHAN // CUTS
-    loads, stores = [], []
-    for i in range(5):
-        for j in range(CUTS):
-            here = (i, 0, pl.ds(j * rows, rows))
-            there = (0, pl.ds(j * rows, rows))
-            loads.append(pltpu.make_async_copy(made[i].at[there], held.at[here], sem_in.at[len(loads)]))
-            stores.append(pltpu.make_async_copy(held.at[here], outs[i].at[there], sem_out.at[len(stores)]))
-    last = pltpu.make_async_copy(sums, turned, sem_in.at[len(loads)])
-    last.start()
-    for load in loads:
-        load.start()
-    last.wait()
+    made, turned, outs, thin, sem = refs[:5], refs[5], refs[6:15], *refs[15:]
+    stores = [pltpu.make_async_copy(made[i], outs[i], sem.at[i]) for i in range(5)]
+    stores += [pltpu.make_async_copy(thin.at[i], outs[5 + i], sem.at[5 + i]) for i in range(4)]
+    for store in stores[:5]:
+        store.start()
     for i in range(4):
         for c in range(4):
             thin[i, :, c * 128 : (c + 1) * 128] = turned[pl.ds(i * 64 + c, ORDER, stride=4), :]
-        stores.append(pltpu.make_async_copy(thin.at[i], outs[5 + i], sem_out.at[len(stores)]))
-        stores[-1].start()
-    for load, store in zip(loads, stores):
-        load.wait()
-        store.start()
+        stores[5 + i].start()
     for store in stores:
         store.wait()
 
@@ -441,15 +416,15 @@
     bf16 = jnp.bfloat16
     shape = value.shape
     anywhere = pl.BlockSpec(memory_space=pl.ANY)
+    inside = pl.BlockSpec(memory_space=pltpu.VMEM)
     made = pl.pallas_call(
         kernel,
-        out_shape=[jax.ShapeDtypeStruct(shape, bf16)] * 5 + [jax.ShapeDtypeStruct((16, 2, 8, 128), f32)],
+        out_shape=[vmem(shape, bf16)] * 5 + [vmem((16, 2, 8, 128), f32)],
         in_specs=[anywhere] * 12,
-        out_specs=[anywhere] * 6,
+        out_specs=[inside] * 6,
         scratch_shapes=[
             vmem((8, CHAN, LOCAL), bf16),
             vmem((4, ORDER, CHAN), f32),
-            vmem((5, CHAN, LOCAL), bf16),
             dma((12,)),
             turned, turned, turned, turned, turned, turned, turned,
             vmem((4, 64, 128), f32),
@@ -468,7 +443,7 @@
             vmem((15, 2, 8, 128), f32),
             vmem((4, 2, 8, 128), f32),
             vmem((2, 8, 128), f32),
-            dma((5,)), dma((5,)), dma((4,)), dma((15,)), dma((15,)), dma((5,)), dma((5,)), dma((3,)), dma((3,)), dma((6,)),
+            dma((5,)), dma((5,)), dma((4,)), dma((15,)), dma((15,)), dma((5,)), dma((5,)), dma((3,)), dma((3,)),
         ],
         compiler_params=pltpu.CompilerParams(
             collective_id=0, has_side_effects=True, vmem_limit_bytes=56 * 1024 * 1024
@@ -483,17 +458,14 @@
     outs = pl.pallas_call(
         hand_over,
         out_shape=[jax.ShapeDtypeStruct(shape, bf16)] * 5 + [thin] * 4,
-        in_specs=[anywhere] * 6,
+        in_specs=[inside] * 6,
         out_specs=[anywhere] * 9,
         scratch_shapes=[
-            vmem((5,) + shape, bf16),
-            vmem((4 * ORDER * 4, 128), f32),
             vmem((4, ORDER, CHAN), f32),
-            dma((5 * CUTS + 1,)),
-            dma((5 * CUTS + 4,)),
+            dma((9,)),
         ],
         name="hand_over",
-    )(*made)
+    )(*(pltpu.with_memory_space_constraint(array, pltpu.VMEM) for array in made))
     return tuple(outs[:5]) + tuple(out.T for out in outs[5:])
 
 

time: 58.1 us -> 56.8 us (0.978)
  Pallas kernels: 56.7 us -> 55.2 us
    pallas_call x1, Pallas kernels: 2.01 us -> 0.95 us  [per_device(): pl.pallas_call(hand_over, out_shape=[jax.ShapeDtypeStruct(shape, bf16)] *...]
where the time goes in v4:
time: 56.8 us; the launch traced here: 55.9 us
  Pallas kernels  55.2 us (97%)
  between operations  0.65 us (1%)
    pallas_call x1, Pallas kernels, per_device(): pl.pallas_call(kernel, out_shape=[vmem(shape, bf16)] * 5 + [vmem((16, 2,...  54.3 us

profile of v4, /device:TPU:6, one launch (start us, length us, event | category | flops | bytes accessed | tf_op | source)
XLA Modules:
  0.0 55.9 jit_solution(9690778060054028697)
XLA Ops:
  0.6 54.3 %hyena_back.1 = (bf16[1,512,128]{2,1,0:T(8,128)(2,1)S(1)}, bf16[1,512,128]{2,1,0:T(8,128)(2,1)S(1)}, bf16[1,512,128]{2,1,0:T(8,128)(2,1)S(1)}, bf16[1,512,128]{2...) custom-call(bf16[1,512,128]{2,1,0:T(8,128)(2,1)} %value.1, ...), custom_call_target="tpu_custom_call" | custom-call | tf_op jit(solution)/shard_map/hyena_back/pallas_call | solution.py:420
  54.9 0.9 %hand_over.1 = (bf16[1,512,128]{2,1,0:T(8,128)(2,1)}, bf16[1,512,128]{2,1,0:T(8,128)(2,1)}, bf16[1,512,128]{2,1,0:T(8,128)(2,1)}, bf16[1,512,128]{2,1,0:T(8,128)...) custom-call(bf16[1,512,128]{2,1,0:T(8,128)(2,1)S(1)} %get-tuple-elem, ...), custom_call_target="tpu_custom_call" | custom-call | tf_op jit(solution)/shard_map/hand_over/pallas_call | solution.py:458

commit v5 on v4

--- a/solution.py
+++ b/solution.py
@@ -12,6 +12,7 @@
 CHAN = 512
 ORDER = 16
 STATE = (8, 8, 128)
+HALF = (4, 8, 128)
 SCALE = 1.0 / math.sqrt(8192.0)
 UNROLL = 8
 
@@ -51,8 +52,9 @@
         pl.semaphore_signal(barrier, inc=1, device_id=at(2, d), device_id_type=MESH)
 
     trecv[...] = jnp.zeros(trecv.shape, jnp.float32)
-    urecv[0] = jnp.zeros(urecv.shape[1:], jnp.float32)
-    vrecv[0] = jnp.zeros(vrecv.shape[1:], jnp.float32)
+    for h in range(2):
+        urecv[h, 0] = jnp.zeros(urecv.shape[2:], jnp.float32)
+        vrecv[h, 0] = jnp.zeros(vrecv.shape[2:], jnp.float32)
 
     for axis in (0, 1):
         for d in (2, 1, 3):
@@ -104,7 +106,6 @@
 
     state = lax.fori_loop(0, LOCAL, first, zero, unroll=UNROLL)
     keep[S2] = state
-    usend[0, 0] = state
 
     for i in range(6, 12):
         loads[i].wait()
@@ -129,13 +130,13 @@
 
     pl.semaphore_wait(barrier, 9)
 
-    def send(axis, buf, recv, ssem, rsem):
+    def send(axis, buf, recv, ssem, rsem, h):
         for d in (2, 1, 3):
             copy = pltpu.make_async_remote_copy(
-                src_ref=buf.at[axis, 0 if axis == 0 else (coords[axis] + d) // 4],
-                dst_ref=recv.at[axis, 3 - d],
-                send_sem=ssem.at[d - 1 if axis == 0 else axis + 2],
-                recv_sem=rsem.at[3 - d if axis == 0 else axis + 2],
+                src_ref=buf.at[h, axis, 0 if axis == 0 else (coords[axis] + d) // 4],
+                dst_ref=recv.at[h, axis, 3 - d],
+                send_sem=ssem.at[5 * h + (d - 1 if axis == 0 else axis + 2)],
+                recv_sem=rsem.at[5 * h + (3 - d if axis == 0 else axis + 2)],
                 device_id=at(axis, d),
                 device_id_type=MESH,
             )
@@ -144,32 +145,25 @@
             else:
                 pl.when(y + d >= 4)(copy.start)
 
-    def arrived(axis, recv, rsem):
+    def arrived(axis, recv, rsem, h):
         if axis:
-            wait_bytes(recv.at[axis], rsem.at[axis + 2])
+            wait_bytes(recv.at[h, axis], rsem.at[5 * h + axis + 2])
         else:
             for d in (1, 2, 3):
                 @pl.when(y + d < 4)
                 def _():
-                    wait_bytes(recv.at[0, d - 1], rsem.at[d - 1])
-
-    def departed(axis, recv, ssem):
+                    wait_bytes(recv.at[h, 0, d - 1], rsem.at[5 * h + d - 1])
+
+    def departed(axis, recv, ssem, h):
         if axis:
-            wait_bytes(recv.at[axis], ssem.at[axis + 2])
+            wait_bytes(recv.at[h, axis], ssem.at[5 * h + axis + 2])
         else:
             for d in (1, 2, 3):
                 @pl.when(y + d >= 4)
                 def _():
-                    wait_bytes(recv.at[0, d - 1], ssem.at[d - 1])
+                    wait_bytes(recv.at[h, 0, d - 1], ssem.at[5 * h + d - 1])
 
     strides = (2048.0, 512.0, 128.0)
-
-    def suffix_merge(axis, recv, rsem, far, rate):
-        arrived(axis, recv, rsem)
-        power = keep[rate + axis]
-        for d in (3, 2, 1):
-            far = recv[axis, d - 1] + power * far
-        return far, power
 
     def spread_signals():
         for d in (2, 1, 3):
@@ -200,7 +194,7 @@
             state = added(line(i), shifted(state, 128.0, powers))
         for k in range(3):
             tsend[k] = state[k]
-        for k in range(15, 0, -1):
+        for k in (10, 6, 9, 14, 11, 7, 5, 13, 2, 8, 3, 15, 4, 1, 12):
             @pl.when(me + k < 16)
             def _():
                 pltpu.make_async_remote_copy(
@@ -234,18 +228,30 @@
             ).start()
         yrecv[z] = ysend[z]
 
-    def back_step(axis, buf, recv, ssem, rsem, own, rate):
-        far = zero if axis == 0 else keep[EU]
-        far, power = suffix_merge(axis, recv, rsem, far, rate)
-        keep[EU] = far
-        if axis < 2:
-            buf[axis + 1, 0] = far
-            buf[axis + 1, 1] = keep[own] + power * far
-            send(axis + 1, buf, recv, ssem, rsem)
-        return far
+    def back_step(axis, buf, recv, ssem, rsem, own, power):
+        for h in range(2):
+            part = pl.ds(4 * h, 4)
+            arrived(axis, recv, rsem, h)
+            scale = keep[power + axis, part]
+            far = recv[h, axis, 2]
+            if axis:
+                far = far + scale * keep[EU, part]
+            for d in (2, 1):
+                far = recv[h, axis, d - 1] + scale * far
+            keep[EU, part] = far
+            if axis < 2:
+                buf[h, axis + 1, 0] = far
+                buf[h, axis + 1, 1] = keep[own, part] + scale * far
+                send(axis + 1, buf, recv, ssem, rsem, h)
+        return keep[EU]
+
+    def begin(state, buf, recv, ssem, rsem):
+        for h in range(2):
+            buf[h, 0, 0] = state[4 * h : 4 * h + 4]
+            send(0, buf, recv, ssem, rsem, h)
 
     spread_signals()
-    send(0, usend, urecv, us_sem, ur_sem)
+    begin(keep[S2], usend, urecv, us_sem, ur_sem)
 
     for axis, step in enumerate(strides):
         keep[POW2 + axis] = jnp.exp(-step * rate2)
@@ -290,8 +296,7 @@
 
     unused, s1 = lax.fori_loop(0, LOCAL, middle, (c2, zero), unroll=UNROLL)
     keep[S1] = s1
-    vsend[0, 0] = s1
-    send(0, vsend, vrecv, vs_sem, vr_sem)
+    begin(s1, vsend, vrecv, vs_sem, vr_sem)
 
     unused, m1, l01, l11 = near(src1_t, sig1_t, decay1)
     back_step(0, vsend, vrecv, vs_sem, vr_sem, S1, POW1)
@@ -378,8 +383,9 @@
 
     wait_bytes(sums_out.at[pl.ds(0, 15)], p_recv.at[2])
     for axis in range(3):
-        departed(axis, urecv, us_sem)
-        departed(axis, vrecv, vs_sem)
+        for h in range(2):
+            departed(axis, urecv, us_sem, h)
+            departed(axis, vrecv, vs_sem, h)
     wait_bytes(nrecv.at[pl.ds(0, 3)], n_sem.at[0])
     wait_bytes(yrecv.at[pl.ds(0, 3)], n_sem.at[2])
     for k in range(1, 16):
@@ -429,21 +435,21 @@
             turned, turned, turned, turned, turned, turned, turned,
             vmem((4, 64, 128), f32),
             vmem((19,) + STATE, f32),
-            vmem((3, 2) + STATE, f32),
-            vmem((3, 3) + STATE, f32),
+            vmem((2, 3, 2) + HALF, f32),
+            vmem((2, 3, 3) + HALF, f32),
             vmem((4, 3, 2, 8, 128), f32),
             vmem((4, 3, 2, 8, 128), f32),
             vmem((3, 2, 8, 128), f32),
             vmem((15, 3, 2, 8, 128), f32),
             vmem((4, 3, 2, 8, 128), f32),
             vmem((4, 3, 2, 8, 128), f32),
-            vmem((3, 2) + STATE, f32),
-            vmem((3, 3) + STATE, f32),
+            vmem((2, 3, 2) + HALF, f32),
+            vmem((2, 3, 3) + HALF, f32),
             vmem((4,) + STATE, f32),
             vmem((15, 2, 8, 128), f32),
             vmem((4, 2, 8, 128), f32),
             vmem((2, 8, 128), f32),
-            dma((5,)), dma((5,)), dma((4,)), dma((15,)), dma((15,)), dma((5,)), dma((5,)), dma((3,)), dma((3,)),
+            dma((10,)), dma((10,)), dma((4,)), dma((15,)), dma((15,)), dma((10,)), dma((10,)), dma((3,)), dma((3,)),
         ],
         compiler_params=pltpu.CompilerParams(
             collective_id=0, has_side_effects=True, vmem_limit_bytes=56 * 1024 * 1024

time: 56.8 us -> 56.7 us (level)
  no operation moved by 1% of the time
where the time goes in v5:
time: 56.7 us; the launch traced here: 56.2 us
  Pallas kernels  55.5 us (98%)
  between operations  0.65 us (1%)
    pallas_call x1, Pallas kernels, per_device(): pl.pallas_call(kernel, out_shape=[vmem(shape, bf16)] * 5 + [vmem((16, 2,...  54.6 us

profile of v5, /device:TPU:6, one launch (start us, length us, event | category | flops | bytes accessed | tf_op | source)
XLA Modules:
  0.0 56.2 jit_solution(17508608369913998800)
XLA Ops:
  0.6 54.6 %hyena_back.1 = (bf16[1,512,128]{2,1,0:T(8,128)(2,1)S(1)}, bf16[1,512,128]{2,1,0:T(8,128)(2,1)S(1)}, bf16[1,512,128]{2,1,0:T(8,128)(2,1)S(1)}, bf16[1,512,128]{2...) custom-call(bf16[1,512,128]{2,1,0:T(8,128)(2,1)} %value.1, ...), custom_call_target="tpu_custom_call" | custom-call | tf_op jit(solution)/shard_map/hyena_back/pallas_call | solution.py:426
  55.2 0.9 %hand_over.1 = (bf16[1,512,128]{2,1,0:T(8,128)(2,1)}, bf16[1,512,128]{2,1,0:T(8,128)(2,1)}, bf16[1,512,128]{2,1,0:T(8,128)(2,1)}, bf16[1,512,128]{2,1,0:T(8,128)...) custom-call(bf16[1,512,128]{2,1,0:T(8,128)(2,1)S(1)} %get-tuple-elem, ...), custom_call_target="tpu_custom_call" | custom-call | tf_op jit(solution)/shard_map/hand_over/pallas_call | solution.py:464

commit v6 on v5

--- a/solution.py
+++ b/solution.py
@@ -14,7 +14,7 @@
 STATE = (8, 8, 128)
 HALF = (4, 8, 128)
 SCALE = 1.0 / math.sqrt(8192.0)
-UNROLL = 8
+UNROLL = 16
 
 (AMP1, RATE1, AMP2, RATE2, S2, M2, L02, L12, ZA2, ZB2, C2, S1, EU, POW1, POW2) = (*range(13), 13, 16)
 

time: 56.7 us -> 57 us (level)
  no operation moved by 1% of the time
where the time goes in v6:
time: 57 us; the launch traced here: 56.2 us
  Pallas kernels  55.6 us (98%)
  between operations  0.65 us (1%)
    pallas_call x1, Pallas kernels, per_device(): pl.pallas_call(kernel, out_shape=[vmem(shape, bf16)] * 5 + [vmem((16, 2,...  54.6 us

profile of v6, /device:TPU:6, one launch (start us, length us, event | category | flops | bytes accessed | tf_op | source)
XLA Modules:
  0.0 56.2 jit_solution(4856086745914647889)
XLA Ops:
  0.6 54.6 %hyena_back.1 = (bf16[1,512,128]{2,1,0:T(8,128)(2,1)S(1)}, bf16[1,512,128]{2,1,0:T(8,128)(2,1)S(1)}, bf16[1,512,128]{2,1,0:T(8,128)(2,1)S(1)}, bf16[1,512,128]{2...) custom-call(bf16[1,512,128]{2,1,0:T(8,128)(2,1)} %value.1, ...), custom_call_target="tpu_custom_call" | custom-call | tf_op jit(solution)/shard_map/hyena_back/pallas_call | solution.py:426
  55.3 0.9 %hand_over.1 = (bf16[1,512,128]{2,1,0:T(8,128)(2,1)}, bf16[1,512,128]{2,1,0:T(8,128)(2,1)}, bf16[1,512,128]{2,1,0:T(8,128)(2,1)}, bf16[1,512,128]{2,1,0:T(8,128)...) custom-call(bf16[1,512,128]{2,1,0:T(8,128)(2,1)S(1)} %get-tuple-elem, ...), custom_call_target="tpu_custom_call" | custom-call | tf_op jit(solution)/shard_map/hand_over/pallas_call | solution.py:464
